TPU v7x, 32 devices: a whole 2x2x4 slice. The times are simulated.
32 devices in a mesh: cases: 2 (over y), blk: 8 (over z, x), state: 2 (over core).
Axes of the slice: x: 2, y: 2, z: 4, core: 2. Of those that a mesh axis runs over, the one named last changes fastest.
Arguments:
- base_real: float32 [32768], P(('cases', 'blk', 'state')), parts along dimension 0, may hold values from -6 to 6
- base_reactive: float32 [32768], P(('cases', 'blk', 'state')), parts along dimension 0, may hold values from 0.2 to 1
- voltage: float32 [32768], P(('cases', 'blk', 'state')), parts along dimension 0, may hold values from 0.9 to 1.1
- rating: float32 [32768], P(('cases', 'blk', 'state')), parts along dimension 0, may hold values from 1 to 4
- monitored: int32 [16384], P(('cases', 'blk', 'state')), parts along dimension 0, may hold values from 0 to 2047, as said below
- tile_ids: int32 [128, 4], P(('cases', 'blk', 'state')), parts along dimension 0, may hold values from -1 to 7, as said below
- tile_values: bfloat16 [128, 4, 128, 128], P(('cases', 'blk', 'state')), parts along dimension 0, may hold values from -0.5 to 0.5
- outage_ids: int32 [16, 128], P(('cases', 'blk')), parts along dimension 0, may hold values from 0 to 2047, as said below
- coupling: bfloat16 [16, 128, 128], P(('cases', 'blk')), parts along dimension 0, may hold values from -0.5 to 0.5
- outage_pairs: int32 [16, 2, 128], P(('cases', 'blk')), parts along dimension 0, may hold values from 0 to 127, as said below
Outputs:
- branch_peak: float32 [16384], P(('cases', 'blk', 'state')), parts along dimension 0
- worst_loading: float32 [16, 128], P(('cases', 'blk'), 'state'), parts along dimension 0
There are 2 independent parts, one for each index of `cases`. A program takes and returns all parts, laid end to end along the dimension named above; each array names one. Nothing has to cross between parts.
Inputs may be any that keep to these rules, and one draw needn't show every extreme that they name: `monitored`: the 1024 entries of one cycle position (entry index // 1024) are distinct. `outage_ids`: each row holds 128 distinct indices. `tile_ids`: each row names between 2 and 4 distinct outage blocks in its first slots and holds -1 in the remaining slots; some row is full. `outage_pairs`: the two branches of a pair differ.
All inputs are finite; a program needn't handle non-finite values.
Results may differ from a plain program's by a relative error of at most 0.0019.
Values may be sent and summed in bfloat16 or wider, within the bound.
A program may use at most 64 MiB of HBM per device.

v0:
```python
import jax
import jax.numpy as jnp
from jax import lax
from jax.sharding import PartitionSpec as P


def solve_pairs(flows_block, coupling_block, pair_block):
    first_idx = pair_block[0]
    second_idx = pair_block[1]
    flow_first = jnp.take(flows_block, first_idx).astype(jnp.float32)
    flow_second = jnp.take(flows_block, second_idx).astype(jnp.float32)
    s_first_second = coupling_block[first_idx, second_idx].astype(jnp.float32)
    s_second_first = coupling_block[second_idx, first_idx].astype(jnp.float32)
    determinant = 1.0 - s_first_second * s_second_first
    w_first = (flow_first + s_first_second * flow_second) / determinant
    w_second = (flow_second + s_second_first * flow_first) / determinant
    return (w_first, w_second)


def body(
    base_real,
    base_reactive,
    voltage,
    rating,
    monitored,
    tile_ids,
    tile_values,
    outage_ids,
    coupling,
    outage_pairs,
):
    real_pos, reactive_pos, volt_pos, rating_pos = (
        lax.all_gather(base_real, "state", axis=0, tiled=True),
        lax.all_gather(base_reactive, "state", axis=0, tiled=True),
        lax.all_gather(voltage, "state", axis=0, tiled=True),
        lax.all_gather(rating, "state", axis=0, tiled=True),
    )
    tiles_dev = tile_ids.shape[0]
    slot_count = tile_ids.shape[1]
    tile_size = tile_values.shape[2]
    pair_count = outage_pairs.shape[2]
    blocks = lax.axis_size("blk")
    halves = lax.axis_size("state")
    half_width = pair_count // halves
    mon_real = jnp.take(real_pos, monitored).reshape(tiles_dev, tile_size)
    mon_reactive = jnp.take(reactive_pos, monitored).reshape(tiles_dev, tile_size)
    mon_limit = (jnp.take(volt_pos, monitored) * jnp.take(rating_pos, monitored)).reshape(
        tiles_dev, tile_size
    )
    react_sq = mon_reactive * mon_reactive
    matches = tile_ids[:, :, None] == jnp.arange(blocks, dtype=jnp.int32)[None, None, :]
    slot_table = jnp.sum(
        jnp.where(matches, jnp.arange(slot_count, dtype=jnp.int32)[None, :, None], 0), axis=1
    )
    present = jnp.any(matches, axis=1)
    outage_flow = jnp.take(real_pos, outage_ids).astype(jnp.bfloat16)
    rows_iota = lax.broadcasted_iota(jnp.int32, (tile_size, pair_count), 0)
    tile_rows = jnp.arange(tiles_dev, dtype=jnp.int32)

    def absorb(running, w_first, w_second, pair_block, block_now):
        weights = (
            jnp.where(rows_iota == pair_block[0][None, :], w_first[None, :], 0.0)
            + jnp.where(rows_iota == pair_block[1][None, :], w_second[None, :], 0.0)
        ).astype(jnp.bfloat16)
        slots = lax.dynamic_index_in_dim(slot_table, block_now, 1, keepdims=False)
        has_tile = lax.dynamic_index_in_dim(present, block_now, 1, keepdims=False)
        chosen = tile_values[tile_rows, slots]
        delta = jnp.einsum("tmi,ip->tmp", chosen, weights, preferred_element_type=jnp.float32)
        delta = jnp.where(has_tile[:, None, None], delta, 0.0)
        post = mon_real[:, :, None] + delta
        loading = jnp.sqrt(post * post + react_sq[:, :, None]) / mon_limit[:, :, None]
        peak_load = jnp.maximum(running[0], jnp.max(loading, axis=2))
        block_max = jnp.max(loading, axis=(0, 1))
        worst_load = lax.dynamic_update_slice(
            running[1], block_max[None, :], (block_now, jnp.int32(0))
        )
        return (peak_load, worst_load)

    initial = (
        jnp.zeros((tiles_dev, tile_size), jnp.float32),
        jnp.zeros((blocks, pair_count), jnp.float32),
    )
    own_first, own_second = solve_pairs(outage_flow[0], coupling[0], outage_pairs[0])
    own_weights = jnp.stack([own_first, own_second])[None]
    weight_shard = lax.all_gather(own_weights, "blk", axis=0, tiled=True)
    pair_shard = lax.all_gather(outage_pairs, "blk", axis=0, tiled=True)

    def one_block(position, carried):
        return absorb(
            carried,
            weight_shard[position, 0],
            weight_shard[position, 1],
            pair_shard[position],
            position,
        )

    peak_load, worst_load = lax.fori_loop(0, weight_shard.shape[0], one_block, initial)
    total_max = lax.pmax(worst_load, ("blk", "state"))
    worst_own = lax.dynamic_slice(
        total_max, (lax.axis_index("blk"), lax.axis_index("state") * half_width), (1, half_width)
    )
    return (peak_load.reshape(-1), worst_own)


def solution(mesh):
    return jax.shard_map(
        body,
        mesh=mesh,
        in_specs=(
            P(("cases", "blk", "state")),
            P(("cases", "blk", "state")),
            P(("cases", "blk", "state")),
            P(("cases", "blk", "state")),
            P(("cases", "blk", "state")),
            P(("cases", "blk", "state"), None),
            P(("cases", "blk", "state"), None, None, None),
            P(("cases", "blk"), None),
            P(("cases", "blk"), None, None),
            P(("cases", "blk"), None, None),
        ),
        out_specs=(P(("cases", "blk", "state")), P(("cases", "blk"), "state")),
        check_vma=False,
    )
```

profile of v0, /device:TPU:0, one launch (start us, length us, event | category | flops | bytes accessed | tf_op | source)
XLA Modules:
  0.0 117.2 jit_solution(10796585060166182035)
XLA Ops:
  0.6 0.8 compare_select_fusion.2
  1.4 0.7 copy-done.5
  2.1 2.1 %all_gather.18 = f32[2048]{0:T(1024)S(1)} all-gather(f32[1024]{0:T(1024)S(1)} %copy-done.5), channel_id=1, replica_groups=mesh['cases'=2,'blk'=8,'state'=2] {'state'}, dimensions={0}, use_global_device_ids=true | all-gather | bytes 12288 | tf_op jit(solution)/shard_map/all_gather | solution.py:33
  4.2 1.1 gather_fusion.1
  5.3 1.2 %gather_fusion.5 = bf16[128]{0:T(256)(128)(2,1)S(1)} fusion(bf16[128]{0:T(256)(128)(2,1)S(1)} %convert_bitcast_fusion, s32[1024]{0:T(1024)S(1)} %get-tuple-element.344), kind=kCustom, calls=%fused_computation.clone | custom fusion | bytes 1024 | tf_op jit(solution)/shard_map/jit(_take)/gather | solution.py:10
  6.6 1.2 %gather_fusion.6 = bf16[128]{0:T(256)(128)(2,1)S(1)} fusion(bf16[128]{0:T(256)(128)(2,1)S(1)} %convert_bitcast_fusion, s32[1024]{0:T(1024)S(1)} %get-tuple-element.343), kind=kCustom, calls=%fused_computation.3.clone | custom fusion | bytes 1024 | tf_op jit(solution)/shard_map/jit(_take)/gather | solution.py:11
  7.9 1.5 %gather_fusion.2 = bf16[128]{0:T(256)(128)(2,1)S(1)} fusion(bf16[128,128]{1,0:T(8,128)(2,1)S(1)} %bitcast.84, s32[128]{0:T(128)S(1)} %get-tuple-element.339), kind=kCustom, calls=%fused_computation.8 | custom fusion | bytes 1536 | tf_op jit(solution)/shard_map/gather | solution.py:12
  9.4 1.5 %gather_fusion.3 = bf16[128]{0:T(256)(128)(2,1)S(1)} fusion(bf16[128,128]{1,0:T(8,128)(2,1)S(1)} %bitcast.85, s32[128]{0:T(128)S(1)} %get-tuple-element.340), kind=kCustom, calls=%fused_computation.9 | custom fusion | bytes 1536 | tf_op jit(solution)/shard_map/gather | solution.py:13
  10.9 22.1 %all-gather.1 = f32[8,2,128]{2,1,0:T(2,128)S(1)} all-gather(f32[1,2,128]{2,1,0:T(2,128)S(1)} %maximum_bitcast_fusion), channel_id=2, replica_groups=mesh['cases'=2,'blk'=8,'state'=2] {'blk'}, dimensions={0}, use_global_device_ids=true | all-gather | bytes 9216 | tf_op jit(solution)/shard_map/all_gather | solution.py:85
  33.1 0.7 copy-done.6
  33.7 1.8 %all_gather.22 = f32[2048]{0:T(1024)S(1)} all-gather(f32[1024]{0:T(1024)S(1)} %copy-done.6), channel_id=1, replica_groups=mesh['cases'=2,'blk'=8,'state'=2] {'state'}, dimensions={0}, use_global_device_ids=true | all-gather | bytes 12288 | tf_op jit(solution)/shard_map/all_gather | solution.py:35
  35.5 3.1 %gather_fusion.8 = f32[512]{0:T(512)S(1)} fusion(f32[2048]{0:T(1024)S(1)} %all_gather.22, s32[1024]{0:T(1024)S(1)} %pad_clamp_fusion.3), kind=kCustom, calls=%fused_computation.5.clone | custom fusion | bytes 6144 | tf_op jit(solution)/shard_map/jit(_take)/gather | solution.py:47
  38.7 1.8 %all_gather.23 = f32[2048]{0:T(1024)S(1)} all-gather(f32[1024]{0:T(1024)S(1)} %copy-done.7), channel_id=1, replica_groups=mesh['cases'=2,'blk'=8,'state'=2] {'state'}, dimensions={0}, use_global_device_ids=true | all-gather | bytes 12288 | tf_op jit(solution)/shard_map/all_gather | solution.py:36
  40.5 3.1 %gather_fusion.9 = f32[512]{0:T(512)S(1)} fusion(f32[2048]{0:T(1024)S(1)} %all_gather.23, s32[1024]{0:T(1024)S(1)} %pad_clamp_fusion.3), kind=kCustom, calls=%fused_computation.6.clone | custom fusion | bytes 6144 | tf_op jit(solution)/shard_map/jit(_take)/gather | solution.py:47
  43.6 3.1 %gather_fusion.4 = f32[512]{0:T(512)S(1)} fusion(f32[2048]{0:T(1024)S(1)} %all_gather.18, s32[1024]{0:T(1024)S(1)} %pad_clamp_fusion.3), kind=kCustom, calls=%fused_computation.1.clone | custom fusion | bytes 6144 | tf_op jit(solution)/shard_map/jit(_take)/gather | solution.py:45
  46.8 1.8 %all_gather.21 = f32[2048]{0:T(1024)S(1)} all-gather(f32[1024]{0:T(1024)S(1)} %copy-done.8), channel_id=1, replica_groups=mesh['cases'=2,'blk'=8,'state'=2] {'state'}, dimensions={0}, use_global_device_ids=true | all-gather | bytes 12288 | tf_op jit(solution)/shard_map/all_gather | solution.py:34
  48.6 3.1 %gather_fusion.7 = f32[512]{0:T(512)S(1)} fusion(f32[2048]{0:T(1024)S(1)} %all_gather.21, s32[1024]{0:T(1024)S(1)} %pad_clamp_fusion.3), kind=kCustom, calls=%fused_computation.4.clone | custom fusion | bytes 6144 | tf_op jit(solution)/shard_map/jit(_take)/gather | solution.py:46
  51.7 16.3 %all_gather.19 = s32[8,2,128]{2,1,0:T(2,128)S(1)} all-gather(s32[1,2,128]{2,1,0:T(2,128)S(1)} %copy-done.2), channel_id=1, replica_groups=mesh['cases'=2,'blk'=8,'state'=2] {'blk'}, dimensions={0}, use_global_device_ids=true | all-gather | bytes 9216 | tf_op jit(solution)/shard_map/all_gather | solution.py:86
  68.0 0.1 select_reduce_fusion
  68.1 0.1 copy.13
  68.2 0.1 fusion.22
  68.3 18.8 %while.17 = (s32[]{:T(128)}, f32[4,128]{1,0:T(4,128)S(1)}, f32[8,128]{1,0:T(8,128)S(1)}, f32[512]{0:T(512)S(1)}, pred[4,8]{1,0:T(4,128)(4,1)S(1)}, /*index=5*/s3...) while((s32[]{:T(128)}, f32[4,128]{1,0:T(4,128)S(1)}, ...), condition=%wide.region_5.8_spmd.clone.clone, body=%wide.region_2.7_spmd.clone.clone.sunk | while | flops 17334688 | bytes 417519 | solution.py:97
  68.3 1.6 %gather_fusion = bf16[4,128,128]{2,1,0:T(8,128)(2,1)S(1)} fusion(bf16[4,4,128,128]{3,2,1,0:T(8,128)(2,1)} %get-tuple-element.456, s32[4]{0:T(128)S(1)} %fusion.36), kind=kCustom, calls=%fused_computation.2.clone.clone.1 | custom fusion | bytes 262176 | tf_op jit(solution)/shard_map/while/body/eval_jaxpr/gather | solution.py:67
  70.1 0.1 copy.16
  70.2 0.4 fusion.38
  70.7 1.6 %gather_fusion = bf16[4,128,128]{2,1,0:T(8,128)(2,1)S(1)} fusion(bf16[4,4,128,128]{3,2,1,0:T(8,128)(2,1)} %get-tuple-element.456, s32[4]{0:T(128)S(1)} %fusion.36), kind=kCustom, calls=%fused_computation.2.clone.clone.1 | custom fusion | bytes 262176 | tf_op jit(solution)/shard_map/while/body/eval_jaxpr/gather | solution.py:67
  72.4 0.1 copy.16
  72.5 0.4 fusion.38
  73.0 1.6 %gather_fusion = bf16[4,128,128]{2,1,0:T(8,128)(2,1)S(1)} fusion(bf16[4,4,128,128]{3,2,1,0:T(8,128)(2,1)} %get-tuple-element.456, s32[4]{0:T(128)S(1)} %fusion.36), kind=kCustom, calls=%fused_computation.2.clone.clone.1 | custom fusion | bytes 262176 | tf_op jit(solution)/shard_map/while/body/eval_jaxpr/gather | solution.py:67
  74.8 0.1 copy.16
  74.9 0.4 fusion.38
  75.4 1.6 %gather_fusion = bf16[4,128,128]{2,1,0:T(8,128)(2,1)S(1)} fusion(bf16[4,4,128,128]{3,2,1,0:T(8,128)(2,1)} %get-tuple-element.456, s32[4]{0:T(128)S(1)} %fusion.36), kind=kCustom, calls=%fused_computation.2.clone.clone.1 | custom fusion | bytes 262176 | tf_op jit(solution)/shard_map/while/body/eval_jaxpr/gather | solution.py:67
  77.1 0.1 copy.16
  77.2 0.4 fusion.38
  77.7 1.6 %gather_fusion = bf16[4,128,128]{2,1,0:T(8,128)(2,1)S(1)} fusion(bf16[4,4,128,128]{3,2,1,0:T(8,128)(2,1)} %get-tuple-element.456, s32[4]{0:T(128)S(1)} %fusion.36), kind=kCustom, calls=%fused_computation.2.clone.clone.1 | custom fusion | bytes 262176 | tf_op jit(solution)/shard_map/while/body/eval_jaxpr/gather | solution.py:67
  79.5 0.1 copy.16
  79.6 0.4 fusion.38
  80.0 1.6 %gather_fusion = bf16[4,128,128]{2,1,0:T(8,128)(2,1)S(1)} fusion(bf16[4,4,128,128]{3,2,1,0:T(8,128)(2,1)} %get-tuple-element.456, s32[4]{0:T(128)S(1)} %fusion.36), kind=kCustom, calls=%fused_computation.2.clone.clone.1 | custom fusion | bytes 262176 | tf_op jit(solution)/shard_map/while/body/eval_jaxpr/gather | solution.py:67
  81.8 0.1 copy.16
  81.9 0.4 fusion.38
  82.4 1.6 %gather_fusion = bf16[4,128,128]{2,1,0:T(8,128)(2,1)S(1)} fusion(bf16[4,4,128,128]{3,2,1,0:T(8,128)(2,1)} %get-tuple-element.456, s32[4]{0:T(128)S(1)} %fusion.36), kind=kCustom, calls=%fused_computation.2.clone.clone.1 | custom fusion | bytes 262176 | tf_op jit(solution)/shard_map/while/body/eval_jaxpr/gather | solution.py:67
  84.1 0.1 copy.16
  84.3 0.4 fusion.38
  84.7 1.6 %gather_fusion = bf16[4,128,128]{2,1,0:T(8,128)(2,1)S(1)} fusion(bf16[4,4,128,128]{3,2,1,0:T(8,128)(2,1)} %get-tuple-element.456, s32[4]{0:T(128)S(1)} %fusion.36), kind=kCustom, calls=%fused_computation.2.clone.clone.1 | custom fusion | bytes 262176 | tf_op jit(solution)/shard_map/while/body/eval_jaxpr/gather | solution.py:67
  86.5 0.1 copy.16
  86.6 0.4 fusion.38
  87.1 29.5 %pmax.7 = f32[8,128]{1,0:T(8,128)S(1)} all-reduce(f32[8,128]{1,0:T(8,128)S(1)} %get-tuple-element.223), channel_id=1, replica_groups=mesh['cases'=2,'blk'=8,'state'=2] {'blk','state'}, use_global_device_ids=true, to_apply=%region_6.9 | all-reduce | flops 1024 | bytes 8192 | tf_op jit(solution)/shard_map/pmax | solution.py:98
  116.6 0.6 dynamic_slice.40
  (87 shorter events, 1.4 us)
Async XLA Ops:
  0.6 7.2 %copy-start = (bf16[1,128,128]{2,1,0:T(8,128)(2,1)S(1)}, bf16[1,128,128]{2,1,0:T(8,128)(2,1)}, u32[]{:S(2)}) copy-start(bf16[1,128,128]{2,1,0:T(8,128)(2,1)} %param.24) | copy-start | bytes 98308
  1.4 0.7 copy-start.5
  2.1 2.1 %copy-start.9 = (s32[1,128]{1,0:T(1,128)S(1)}, s32[1,128]{1,0:T(1,128)}, u32[]{:S(2)}) copy-start(s32[1,128]{1,0:T(1,128)} %param.23) | copy-start | bytes 1540
  6.6 1.3 %copy-start.2 = (s32[1,2,128]{2,1,0:T(2,128)S(1)}, s32[1,2,128]{2,1,0:T(2,128)}, u32[]{:S(2)}) copy-start(s32[1,2,128]{2,1,0:T(2,128)} %param.25) | copy-start | bytes 3076
  10.9 22.1 %copy-start.3 = (s32[512]{0:T(512)S(1)}, s32[512]{0:T(512)}, u32[]{:S(2)}) copy-start(s32[512]{0:T(512)} %param.20) | copy-start | bytes 6148
  33.0 0.7 copy-start.6
  35.5 3.1 %copy-start.7 = (f32[1024]{0:T(1024)S(1)}, f32[1024]{0:T(1024)}, u32[]{:S(2)}) copy-start(f32[1024]{0:T(1024)} %param.19) | copy-start | bytes 12292
  43.6 3.2 %copy-start.8 = (f32[1024]{0:T(1024)S(1)}, f32[1024]{0:T(1024)}, u32[]{:S(2)}) copy-start(f32[1024]{0:T(1024)} %param.17) | copy-start | bytes 12292
  51.7 16.3 %copy-start.4 = (s32[4,4]{1,0:T(4,128)S(1)}, s32[4,4]{1,0:T(4,128)}, u32[]{:S(2)}) copy-start(s32[4,4]{1,0:T(4,128)} %param.21) | copy-start | bytes 196
  87.1 29.5 %copy-start.1 = (f32[4,128]{1,0:T(4,128)}, f32[4,128]{1,0:T(4,128)S(1)}, u32[]{:S(2)}) copy-start(f32[4,128]{1,0:T(4,128)S(1)} %get-tuple-element.222) | copy-start | bytes 6148
where the time goes:
time: 118 us; the launch traced here: 117 us
  blocking collectives  75.3 us (64%)
  local copies, waits for them, and re-layouts  36.2 us (31%)
  matrix products  3.15 us (3%)
  other arithmetic  1.22 us (1%)
    pmax x1, blocking collectives, body(): total_max = lax.pmax(worst_load, ('blk', 'state'))  29.5 us
    all_gather x1, blocking collectives, body(): weight_shard = lax.all_gather(own_weights, 'blk', axis=0, tiled=True)  22.1 us
    all_gather x1, blocking collectives, body(): pair_shard = lax.all_gather(outage_pairs, 'blk', axis=0, tiled=True)  16.3 us
    gather x8, local copies, waits for them, and re-layouts, absorb(): chosen = tile_values[tile_rows, slots]  12.9 us
    dot_general x8, matrix products, absorb(): jnp.einsum('tmi,ip->tmp', chosen, weights, preferred_element_type=jnp.flo...  3.15 us
    gather x1, local copies, waits for them, and re-layouts, body(): mon_real = jnp.take(real_pos, monitored).reshape(tiles_dev, tile_size)  3.14 us
    gather x1, local copies, waits for them, and re-layouts, body(): jnp.take(volt_pos, monitored) * jnp.take(rating_pos, monitored)  3.13 us
    gather x1, local copies, waits for them, and re-layouts, body(): jnp.take(reactive_pos, monitored).reshape(tiles_dev, tile_size)  3.13 us

commit v1 on v0

v1 whole, which is shorter than its diff:
```python
import functools

import jax
import jax.numpy as jnp
from jax import lax
from jax.experimental import pallas as pl
from jax.experimental.pallas import tpu as pltpu
from jax.sharding import PartitionSpec as P

MESH = pl.DeviceIdType.MESH
LANES = 128


def take_lanes(row, lanes):
    spread = jnp.broadcast_to(row, lanes.shape)
    return jnp.take_along_axis(spread, lanes, axis=1, mode="promise_in_bounds")


def lookup(table, high, low, first_row):
    found = jnp.zeros(low.shape, table.dtype)
    for r in range(table.shape[0]):
        found = jnp.where(high == first_row + r, take_lanes(table[r : r + 1], low), found)
    return found


def each(count, step, unrolled):
    if unrolled:
        for i in range(count):
            step(i)
    else:

        def one(i, carry):
            step(i)
            return carry

        lax.fori_loop(0, count, one, 0)


def kernel(
    blocks,
    halves,
    ids_ref,
    real_ref,
    react_ref,
    volt_ref,
    rating_ref,
    mon_ref,
    out_ids_ref,
    pairs_ref,
    coup_ref,
    tiles_hbm,
    peak_ref,
    worst_ref,
    tiles,
    index,
    table_out,
    table_in,
    pair_out,
    pair_in,
    weights,
    columns,
    rows,
    squares,
    worst_out,
    worst_in,
    tile_sem,
    table_sems,
    pair_send,
    pair_recv,
    worst_send,
    worst_recv,
):
    devices = blocks * halves
    tiles_dev, slots, tile_size, _ = tiles_hbm.shape
    table_rows = real_ref.shape[0]
    unrolled = devices <= 16
    blk = lax.axis_index("blk")
    state = lax.axis_index("state")
    me = state * blocks + blk

    def place(i):
        other = lax.rem(me + i + 1, devices)
        return other, {"blk": lax.rem(other, blocks), "state": other // blocks}

    barrier = pltpu.get_barrier_semaphore()

    def greet(i):
        _, where_to = place(i)
        pl.semaphore_signal(barrier, inc=1, device_id=where_to, device_id_type=MESH)

    each(devices - 1, greet, unrolled)
    tile_copy = pltpu.make_async_copy(tiles_hbm, tiles, tile_sem)
    tile_copy.start()

    first, second = pairs_ref[0:1], pairs_ref[1:2]
    spot = lax.broadcasted_iota(jnp.int32, (tile_size, first.shape[1]), 0)
    at_first, at_second = spot == first, spot == second
    one, zero = jnp.float32(1.0), jnp.float32(0.0)
    picks = jnp.concatenate([jnp.where(at_second, one, zero), jnp.where(at_first, one, zero)], axis=1)
    picked = jnp.dot(coup_ref[...], picks.astype(jnp.bfloat16), preferred_element_type=jnp.float32)
    pair_count = first.shape[1]
    s_first_second = jnp.sum(jnp.where(at_first, picked[:, :pair_count], 0.0), axis=0, keepdims=True)
    s_second_first = jnp.sum(jnp.where(at_second, picked[:, pair_count:], 0.0), axis=0, keepdims=True)

    index[...] = jnp.zeros_like(index)
    index[0:tiles_dev] = mon_ref[...]
    out_ids = out_ids_ref[...]
    wide = (8, LANES)
    index[tiles_dev : tiles_dev + 1] = take_lanes(out_ids, jnp.broadcast_to(first, wide))[0:1]
    index[tiles_dev + 1 : tiles_dev + 2] = take_lanes(out_ids, jnp.broadcast_to(second, wide))[0:1]
    high, low = index[...] >> 7, index[...] & (LANES - 1)

    limit_own = volt_ref[...] * rating_ref[...]
    table_out[0] = real_ref[...]
    table_out[1] = react_ref[...]
    table_out[2] = limit_own
    own_row = state * table_rows
    real_own = lookup(real_ref[...], high, low, own_row)
    flows = real_own[tiles_dev : tiles_dev + 2].astype(jnp.bfloat16).astype(jnp.float32)
    is_first = state == 0
    pair_out[0:2] = flows
    pair_out[2:3] = jnp.where(is_first, first.astype(jnp.float32), s_first_second)
    pair_out[3:4] = jnp.where(is_first, second.astype(jnp.float32), s_second_first)

    pl.semaphore_wait(barrier, devices - 1)

    def pair_copy(i):
        other, where_to = place(i)
        return pltpu.make_async_remote_copy(
            src_ref=pair_out,
            dst_ref=pair_in.at[me],
            send_sem=pair_send.at[other],
            recv_sem=pair_recv.at[me],
            device_id=where_to,
            device_id_type=MESH,
        )

    table_copy = pltpu.make_async_remote_copy(
        src_ref=table_out,
        dst_ref=table_in,
        send_sem=table_sems.at[0],
        recv_sem=table_sems.at[1],
        device_id={"state": 1 - state},
        device_id_type=MESH,
    )
    each(devices - 1, lambda i: pair_copy(i).start(), unrolled)
    table_copy.start()
    pair_in[me] = pair_out[...]

    react_own = lookup(react_ref[...], high, low, own_row)
    limit_mine = lookup(limit_own, high, low, own_row)
    weights[0] = jnp.zeros(weights.shape[1:], weights.dtype)
    table_copy.wait_recv()
    other_row = (1 - state) * table_rows
    mine = (high >= own_row) & (high < own_row + table_rows)
    real = jnp.where(mine, real_own, lookup(table_in[0], high, low, other_row))
    react = jnp.where(mine, react_own, lookup(table_in[1], high, low, other_row))
    limit = jnp.where(mine, limit_mine, lookup(table_in[2], high, low, other_row))
    react_sq = react * react
    rows[0:8] = real
    rows[8:16] = react_sq
    rows[16:24] = 1.0 / (limit * limit)
    rows[24:] = jnp.zeros((rows.shape[0] - 24, LANES), jnp.float32)
    upright = rows[...].T
    for t in range(tiles_dev):
        for q in range(3):
            column = upright[:, 8 * q + t : 8 * q + t + 1]
            columns[t, q] = jnp.broadcast_to(column, (tile_size, pair_count))
    block_of = lax.broadcasted_iota(jnp.int32, (blocks, pair_count), 0)
    worst = jnp.zeros((blocks, pair_count), jnp.float32)
    for t in range(tiles_dev):
        base = columns[t, 0]
        base_peak = jnp.max((base * base + columns[t, 1]) * columns[t, 2], axis=0, keepdims=True)
        absent = block_of >= 0
        for k in range(slots):
            absent = absent & (block_of != ids_ref[t, k])
        worst = jnp.maximum(worst, jnp.where(absent, base_peak, 0.0))
    tile_copy.wait()

    def pair_arrived(i):
        other, where_to = place(i)
        pltpu.make_async_remote_copy(
            src_ref=pair_out,
            dst_ref=pair_in.at[other],
            send_sem=pair_send.at[other],
            recv_sem=pair_recv.at[other],
            device_id=where_to,
            device_id_type=MESH,
        ).wait_recv()

    each(devices - 1, pair_arrived, unrolled)
    flow_first = pair_in[0:blocks, 0] + pair_in[blocks:, 0]
    flow_second = pair_in[0:blocks, 1] + pair_in[blocks:, 1]
    first_all = pair_in[0:blocks, 2].astype(jnp.int32)
    second_all = pair_in[0:blocks, 3].astype(jnp.int32)
    s_fs, s_sf = pair_in[blocks:, 2], pair_in[blocks:, 3]
    determinant = 1.0 - s_fs * s_sf
    w_first = (flow_first + s_fs * flow_second) / determinant
    w_second = (flow_second + s_sf * flow_first) / determinant
    for b in range(blocks):
        one_row = slice(b, b + 1)
        weights[b + 1] = jnp.where(
            spot == first_all[one_row],
            w_first[one_row],
            jnp.where(spot == second_all[one_row], w_second[one_row], 0.0),
        ).astype(jnp.bfloat16)

    for t in range(tiles_dev):

        def one_slot(k, carried):
            most, worst = carried
            block = ids_ref[t, k]
            delta = jnp.dot(tiles[t, k], weights[block + 1], preferred_element_type=jnp.float32)
            post = columns[t, 0] + delta
            square = post * post
            ratio = (square + columns[t, 1]) * columns[t, 2]
            top = jnp.max(ratio, axis=0, keepdims=True)
            worst = jnp.where(block_of == block, jnp.maximum(worst, top), worst)
            return jnp.maximum(most, square), worst

        base = columns[t, 0]
        carried = (base * base, worst)
        if slots <= 4:
            for k in range(slots):
                carried = one_slot(k, carried)
        else:
            carried = lax.fori_loop(0, slots, one_slot, carried)
        most, worst = carried
        squares[t] = most
    worst_out[:, 0] = worst

    def worst_copy(i):
        other, where_to = place(i)
        return pltpu.make_async_remote_copy(
            src_ref=worst_out.at[where_to["blk"]],
            dst_ref=worst_in.at[me],
            send_sem=worst_send.at[other],
            recv_sem=worst_recv.at[me],
            device_id=where_to,
            device_id_type=MESH,
        )

    each(devices - 1, lambda i: worst_copy(i).start(), unrolled)
    worst_in[me] = worst_out[blk]
    for t in range(tiles_dev):
        most = jnp.max(squares[t].T, axis=0, keepdims=True)
        peak_ref[t : t + 1] = jnp.sqrt((most + rows[8 + t : 9 + t]) * rows[16 + t : 17 + t])

    def worst_arrived(i):
        other, where_to = place(i)
        pltpu.make_async_remote_copy(
            src_ref=worst_out.at[blk],
            dst_ref=worst_in.at[other],
            send_sem=worst_send.at[other],
            recv_sem=worst_recv.at[other],
            device_id=where_to,
            device_id_type=MESH,
        ).wait_recv()

    each(devices - 1, worst_arrived, unrolled)
    total = jnp.sqrt(jnp.max(worst_in[...], axis=0))
    half = pair_count // halves
    worst_ref[...] = jnp.where(is_first, total[:, :half], total[:, half:])

    table_copy.wait_send()

    def sent(i):
        pair_copy(i).wait_send()
        worst_copy(i).wait_send()

    each(devices - 1, sent, unrolled)


def body(
    base_real,
    base_reactive,
    voltage,
    rating,
    monitored,
    tile_ids,
    tile_values,
    outage_ids,
    coupling,
    outage_pairs,
):
    blocks = lax.axis_size("blk")
    halves = lax.axis_size("state")
    devices = blocks * halves
    tiles_dev, slots, tile_size, _ = tile_values.shape
    pair_count = outage_pairs.shape[2]
    table_rows = base_real.shape[0] // LANES
    vmem = pl.BlockSpec(memory_space=pltpu.VMEM)
    f32 = jnp.float32
    peak, worst = pl.pallas_call(
        functools.partial(kernel, blocks, halves),
        out_shape=(
            jax.ShapeDtypeStruct((tiles_dev, tile_size), f32),
            jax.ShapeDtypeStruct((1, pair_count // halves), f32),
        ),
        in_specs=[pl.BlockSpec(memory_space=pltpu.SMEM)]
        + [vmem] * 8
        + [pl.BlockSpec(memory_space=pl.ANY)],
        out_specs=(vmem, vmem),
        scratch_shapes=[
            pltpu.VMEM(tile_values.shape, tile_values.dtype),
            pltpu.VMEM((8, LANES), jnp.int32),
            pltpu.VMEM((3, table_rows, LANES), f32),
            pltpu.VMEM((3, table_rows, LANES), f32),
            pltpu.VMEM((4, pair_count), f32),
            pltpu.VMEM((devices, 4, pair_count), f32),
            pltpu.VMEM((blocks + 1, tile_size, pair_count), jnp.bfloat16),
            pltpu.VMEM((tiles_dev, 3, tile_size, pair_count), f32),
            pltpu.VMEM((LANES, LANES), f32),
            pltpu.VMEM((tiles_dev, tile_size, pair_count), f32),
            pltpu.VMEM((blocks, 1, pair_count), f32),
            pltpu.VMEM((devices, 1, pair_count), f32),
            pltpu.SemaphoreType.DMA(()),
            pltpu.SemaphoreType.DMA((2,)),
            pltpu.SemaphoreType.DMA((devices,)),
            pltpu.SemaphoreType.DMA((devices,)),
            pltpu.SemaphoreType.DMA((devices,)),
            pltpu.SemaphoreType.DMA((devices,)),
        ],
        compiler_params=pltpu.CompilerParams(
            collective_id=0, has_side_effects=True, vmem_limit_bytes=48 * 1024 * 1024
        ),
        name="screen",
    )(
        tile_ids,
        base_real.reshape(table_rows, LANES),
        base_reactive.reshape(table_rows, LANES),
        voltage.reshape(table_rows, LANES),
        rating.reshape(table_rows, LANES),
        monitored.reshape(tiles_dev, tile_size),
        outage_ids,
        outage_pairs[0],
        coupling[0],
        tile_values,
    )
    return peak.reshape(-1), worst


def solution(mesh):
    every = P(("cases", "blk", "state"))
    by_block = P(("cases", "blk"))
    return jax.shard_map(
        body,
        mesh=mesh,
        in_specs=(every,) * 7 + (by_block,) * 3,
        out_specs=(every, P(("cases", "blk"), "state")),
        check_vma=False,
    )
```

time: 118 us -> 23.4 us (0.20)
  blocking collectives: 75.3 us -> 0 us
  local copies, waits for them, and re-layouts: 36.2 us -> 6.29 us
  Pallas kernels: 0 us -> 16 us
  matrix products: 3.15 us -> 0 us
  other arithmetic: 1.22 us -> 0 us
    all_gather x6 -> x0, blocking collectives: 45.8 us -> none  [the longest x1 22.1 us: body(): weight_shard = lax.all_gather(own_weights, 'blk', axis=0, tiled=True)]
    gather x17 -> x0, local copies, waits for them, and re-layouts: 32.1 us -> none  [the longest x8 12.9 us: absorb(): chosen = tile_values[tile_rows, slots]]
    pmax x1 -> x0, blocking collectives: 29.5 us -> none  [body(): total_max = lax.pmax(worst_load, ('blk', 'state'))]
    pallas_call x0 -> x1, Pallas kernels: none -> 16 us  [body(): pl.pallas_call(functools.partial(kernel, blocks, halves), out_shape=(jax....]
    unnamed x21 -> x22, local copies, waits for them, and re-layouts: 1.48 us -> 6.29 us
    dot_general x8 -> x0, matrix products: 3.15 us -> none  [absorb(): jnp.einsum('tmi,ip->tmp', chosen, weights, preferred_element_type=jnp.flo...]
    dynamic_slice x25 -> x0, local copies, waits for them, and re-layouts: 2.18 us -> none  [the longest x16 1.51 us: absorb(): has_tile = lax.dynamic_index_in_dim(present, block_now, 1, keepdims=False)]
where the time goes in v1:
time: 23.4 us; the launch traced here: 23 us
  Pallas kernels  16 us (68%)
  local copies, waits for them, and re-layouts  6.29 us (27%)
  between operations  0.68 us (3%)
    pallas_call x1, Pallas kernels, body(): pl.pallas_call(functools.partial(kernel, blocks, halves), out_shape=(jax....  16 us
    unnamed x22, local copies, waits for them, and re-layouts  6.29 us

profile of v1, /device:TPU:0, one launch (start us, length us, event | category | flops | bytes accessed | tf_op | source)
XLA Modules:
  0.0 23.0 jit_solution(9093264959727339938)
XLA Ops:
  0.6 0.0 copy-start.4
  0.6 0.0 copy-start.3
  0.7 0.0 copy-start.2
  0.7 0.0 copy-start.8
  0.7 0.6 %copy-done.4 = f32[1024]{0:T(1024)S(1)} copy-done((f32[1024]{0:T(1024)S(1)}, f32[1024]{0:T(1024)}, u32[]{:S(2)}) %copy-start.4) | copy-done | bytes 4120
  1.3 0.0 copy-done.3
  1.3 0.0 copy-done.2
  1.4 0.0 copy-done.8
  1.4 0.0 copy-start
  1.4 1.0 %copy-done = bf16[4,4,128,128]{3,2,1,0:T(8,128)(2,1)S(1)} copy-done((bf16[4,4,128,128]{3,2,1,0:T(8,128)(2,1)S(1)}, bf16[4,4,128,128]{3,2,1,0:T(8,128)(2,1)}, u32[]{:S(2)}) %copy-start) | copy-done | bytes 524312
  2.4 0.0 copy-start.1
  2.4 0.8 %copy-done.1 = bf16[1,128,128]{2,1,0:T(8,128)(2,1)S(1)} copy-done((bf16[1,128,128]{2,1,0:T(8,128)(2,1)S(1)}, bf16[1,128,128]{2,1,0:T(8,128)(2,1)}, u32[]{:S(2)}) %copy-start.1) | copy-done | bytes 32792
  3.2 0.0 copy-start.5
  3.2 0.7 %copy-done.5 = f32[1024]{0:T(1024)S(1)} copy-done((f32[1024]{0:T(1024)S(1)}, f32[1024]{0:T(1024)}, u32[]{:S(2)}) %copy-start.5) | copy-done | bytes 4120
  3.8 0.0 copy-start.6
  3.9 0.7 %copy-done.6 = s32[4,4]{1,0:T(4,128)S(1)} copy-done((s32[4,4]{1,0:T(4,128)S(1)}, s32[4,4]{1,0:T(4,128)}, u32[]{:S(2)}) %copy-start.6) | copy-done | bytes 88
  4.5 0.0 copy-start.7
  4.5 0.7 %copy-done.7 = s32[512]{0:T(512)S(1)} copy-done((s32[512]{0:T(512)S(1)}, s32[512]{0:T(512)}, u32[]{:S(2)}) %copy-start.7) | copy-done | bytes 2072
  5.2 0.0 copy-start.9
  5.2 0.7 %copy-done.9 = s32[1,128]{1,0:T(1,128)S(1)} copy-done((s32[1,128]{1,0:T(1,128)S(1)}, s32[1,128]{1,0:T(1,128)}, u32[]{:S(2)}) %copy-start.9) | copy-done | bytes 536
  5.9 16.0 %screen.1 = (f32[4,128]{1,0:T(4,128)S(1)}, f32[1,64]{1,0:T(1,128)S(1)}) custom-call(s32[4,4]{1,0:T(4,128)S(1)} %copy-done.6, f32[8,128]{1,0:T(8,128)S(1)} %bitcast.9, f32[8,128]{1,0:T(8,128)S(1)} %bitcast.10, f32[8,128]{1,0:T(8,128)S(1)} %bitcast.11, f32[8,128]{1,0:T(8,128)S(1)} %bitcast.12, s32[4,128]{1,0:T(4,128)S(1)} %bitcast.13, s32[1,128]{1,0:T(1,128)S(1)} %copy-done.9, ...), custom_call_target="tpu_custom_call" | custom-call | tf_op jit(solution)/shard_map/screen/pallas_call | solution.py:294
  21.9 0.6 %copy.14 = f32[512]{0:T(512)} copy(f32[512]{0:T(512)S(1)} %bitcast.14) | data formatting | bytes 4096
  22.5 0.5 %copy.15 = f32[1,64]{1,0:T(1,128)} copy(f32[1,64]{1,0:T(1,128)S(1)} %get-tuple-element.9) | data formatting | bytes 512
Async XLA Ops:
  0.6 0.7 %copy-start.4 = (f32[1024]{0:T(1024)S(1)}, f32[1024]{0:T(1024)}, u32[]{:S(2)}) copy-start(f32[1024]{0:T(1024)} %param.12) | copy-start | bytes 12292
  0.6 0.7 %copy-start.3 = (f32[1024]{0:T(1024)S(1)}, f32[1024]{0:T(1024)}, u32[]{:S(2)}) copy-start(f32[1024]{0:T(1024)} %param.11) | copy-start | bytes 12292
  0.7 0.7 %copy-start.2 = (f32[1024]{0:T(1024)S(1)}, f32[1024]{0:T(1024)}, u32[]{:S(2)}) copy-start(f32[1024]{0:T(1024)} %param.10) | copy-start | bytes 12292
  0.7 0.7 %copy-start.8 = (s32[1,2,128]{2,1,0:T(2,128)S(1)}, s32[1,2,128]{2,1,0:T(2,128)}, u32[]{:S(2)}) copy-start(s32[1,2,128]{2,1,0:T(2,128)} %param.19) | copy-start | bytes 3076
  1.4 1.0 %copy-start = (bf16[4,4,128,128]{3,2,1,0:T(8,128)(2,1)S(1)}, bf16[4,4,128,128]{3,2,1,0:T(8,128)(2,1)}, u32[]{:S(2)}) copy-start(bf16[4,4,128,128]{3,2,1,0:T(8,128)(2,1)} %tiles_hbm.1) | copy-start | bytes 1572868
  2.4 0.8 %copy-start.1 = (bf16[1,128,128]{2,1,0:T(8,128)(2,1)S(1)}, bf16[1,128,128]{2,1,0:T(8,128)(2,1)}, u32[]{:S(2)}) copy-start(bf16[1,128,128]{2,1,0:T(8,128)(2,1)} %param.18) | copy-start | bytes 98308
  3.2 0.7 %copy-start.5 = (f32[1024]{0:T(1024)S(1)}, f32[1024]{0:T(1024)}, u32[]{:S(2)}) copy-start(f32[1024]{0:T(1024)} %param.13) | copy-start | bytes 12292
  3.8 0.7 %copy-start.6 = (s32[4,4]{1,0:T(4,128)S(1)}, s32[4,4]{1,0:T(4,128)}, u32[]{:S(2)}) copy-start(s32[4,4]{1,0:T(4,128)} %ids_ref.1) | copy-start | bytes 196
  4.5 0.7 %copy-start.7 = (s32[512]{0:T(512)S(1)}, s32[512]{0:T(512)}, u32[]{:S(2)}) copy-start(s32[512]{0:T(512)} %param.14) | copy-start | bytes 6148
  5.2 0.7 %copy-start.9 = (s32[1,128]{1,0:T(1,128)S(1)}, s32[1,128]{1,0:T(1,128)}, u32[]{:S(2)}) copy-start(s32[1,128]{1,0:T(1,128)} %out_ids_ref.1) | copy-start | bytes 1540

commit v2 on v1

--- a/solution.py
+++ b/solution.py
@@ -39,18 +39,26 @@
 def kernel(
     blocks,
     halves,
-    ids_ref,
+    pairs_hbm,
+    coup_hbm,
+    out_ids_hbm,
+    real_hbm,
+    mon_hbm,
+    react_hbm,
+    volt_hbm,
+    rating_hbm,
+    ids_hbm,
+    tiles_hbm,
+    out_ref,
+    pairs_ref,
+    coup_ref,
+    out_ids_ref,
     real_ref,
+    mon_ref,
     react_ref,
     volt_ref,
     rating_ref,
-    mon_ref,
-    out_ids_ref,
-    pairs_ref,
-    coup_ref,
-    tiles_hbm,
-    peak_ref,
-    worst_ref,
+    ids_ref,
     tiles,
     index,
     table_out,
@@ -63,7 +71,7 @@
     squares,
     worst_out,
     worst_in,
-    tile_sem,
+    load_sems,
     table_sems,
     pair_send,
     pair_recv,
@@ -82,6 +90,25 @@
         other = lax.rem(me + i + 1, devices)
         return other, {"blk": lax.rem(other, blocks), "state": other // blocks}
 
+    loads = [
+        pltpu.make_async_copy(source, target, load_sems.at[i])
+        for i, (source, target) in enumerate(
+            (
+                (pairs_hbm, pairs_ref),
+                (coup_hbm, coup_ref),
+                (out_ids_hbm, out_ids_ref),
+                (real_hbm, real_ref),
+                (mon_hbm, mon_ref),
+                (react_hbm, react_ref),
+                (volt_hbm, volt_ref),
+                (rating_hbm, rating_ref),
+                (ids_hbm, ids_ref),
+                (tiles_hbm, tiles),
+            )
+        )
+    ]
+    for load in loads[:8]:
+        load.start()
     barrier = pltpu.get_barrier_semaphore()
 
     def greet(i):
@@ -89,8 +116,10 @@
         pl.semaphore_signal(barrier, inc=1, device_id=where_to, device_id_type=MESH)
 
     each(devices - 1, greet, unrolled)
-    tile_copy = pltpu.make_async_copy(tiles_hbm, tiles, tile_sem)
-    tile_copy.start()
+    for load in loads[8:]:
+        load.start()
+    for load in loads[:8]:
+        load.wait()
 
     first, second = pairs_ref[0:1], pairs_ref[1:2]
     spot = lax.broadcasted_iota(jnp.int32, (tile_size, first.shape[1]), 0)
@@ -166,6 +195,7 @@
         for q in range(3):
             column = upright[:, 8 * q + t : 8 * q + t + 1]
             columns[t, q] = jnp.broadcast_to(column, (tile_size, pair_count))
+    loads[8].wait()
     block_of = lax.broadcasted_iota(jnp.int32, (blocks, pair_count), 0)
     worst = jnp.zeros((blocks, pair_count), jnp.float32)
     for t in range(tiles_dev):
@@ -175,7 +205,7 @@
         for k in range(slots):
             absent = absent & (block_of != ids_ref[t, k])
         worst = jnp.maximum(worst, jnp.where(absent, base_peak, 0.0))
-    tile_copy.wait()
+    loads[9].wait()
 
     def pair_arrived(i):
         other, where_to = place(i)
@@ -244,7 +274,7 @@
     worst_in[me] = worst_out[blk]
     for t in range(tiles_dev):
         most = jnp.max(squares[t].T, axis=0, keepdims=True)
-        peak_ref[t : t + 1] = jnp.sqrt((most + rows[8 + t : 9 + t]) * rows[16 + t : 17 + t])
+        out_ref[t : t + 1] = jnp.sqrt((most + rows[8 + t : 9 + t]) * rows[16 + t : 17 + t])
 
     def worst_arrived(i):
         other, where_to = place(i)
@@ -260,7 +290,7 @@
     each(devices - 1, worst_arrived, unrolled)
     total = jnp.sqrt(jnp.max(worst_in[...], axis=0))
     half = pair_count // halves
-    worst_ref[...] = jnp.where(is_first, total[:, :half], total[:, half:])
+    out_ref[tiles_dev : tiles_dev + 1, :half] = jnp.where(is_first, total[:, :half], total[:, half:])
 
     table_copy.wait_send()
 
@@ -289,20 +319,27 @@
     tiles_dev, slots, tile_size, _ = tile_values.shape
     pair_count = outage_pairs.shape[2]
     table_rows = base_real.shape[0] // LANES
-    vmem = pl.BlockSpec(memory_space=pltpu.VMEM)
     f32 = jnp.float32
-    peak, worst = pl.pallas_call(
+    operands = (
+        outage_pairs[0],
+        coupling[0],
+        outage_ids,
+        base_real.reshape(table_rows, LANES),
+        monitored.reshape(tiles_dev, tile_size),
+        base_reactive.reshape(table_rows, LANES),
+        voltage.reshape(table_rows, LANES),
+        rating.reshape(table_rows, LANES),
+        tile_ids,
+        tile_values,
+    )
+    spaces = [pltpu.VMEM] * 8 + [pltpu.SMEM, pltpu.VMEM]
+    results = pl.pallas_call(
         functools.partial(kernel, blocks, halves),
-        out_shape=(
-            jax.ShapeDtypeStruct((tiles_dev, tile_size), f32),
-            jax.ShapeDtypeStruct((1, pair_count // halves), f32),
-        ),
-        in_specs=[pl.BlockSpec(memory_space=pltpu.SMEM)]
-        + [vmem] * 8
-        + [pl.BlockSpec(memory_space=pl.ANY)],
-        out_specs=(vmem, vmem),
-        scratch_shapes=[
-            pltpu.VMEM(tile_values.shape, tile_values.dtype),
+        out_shape=jax.ShapeDtypeStruct((8, LANES), f32),
+        in_specs=[pl.BlockSpec(memory_space=pltpu.HBM)] * 10,
+        out_specs=pl.BlockSpec(memory_space=pltpu.VMEM),
+        scratch_shapes=[space(x.shape, x.dtype) for space, x in zip(spaces, operands)]
+        + [
             pltpu.VMEM((8, LANES), jnp.int32),
             pltpu.VMEM((3, table_rows, LANES), f32),
             pltpu.VMEM((3, table_rows, LANES), f32),
@@ -314,7 +351,7 @@
             pltpu.VMEM((tiles_dev, tile_size, pair_count), f32),
             pltpu.VMEM((blocks, 1, pair_count), f32),
             pltpu.VMEM((devices, 1, pair_count), f32),
-            pltpu.SemaphoreType.DMA(()),
+            pltpu.SemaphoreType.DMA((10,)),
             pltpu.SemaphoreType.DMA((2,)),
             pltpu.SemaphoreType.DMA((devices,)),
             pltpu.SemaphoreType.DMA((devices,)),
@@ -322,22 +359,13 @@
             pltpu.SemaphoreType.DMA((devices,)),
         ],
         compiler_params=pltpu.CompilerParams(
-            collective_id=0, has_side_effects=True, vmem_limit_bytes=48 * 1024 * 1024
+            collective_id=0, has_side_effects=True, vmem_limit_bytes=64 * 1024 * 1024
         ),
         name="screen",
-    )(
-        tile_ids,
-        base_real.reshape(table_rows, LANES),
-        base_reactive.reshape(table_rows, LANES),
-        voltage.reshape(table_rows, LANES),
-        rating.reshape(table_rows, LANES),
-        monitored.reshape(tiles_dev, tile_size),
-        outage_ids,
-        outage_pairs[0],
-        coupling[0],
-        tile_values,
-    )
-    return peak.reshape(-1), worst
+    )(*operands)
+    peak = results[:tiles_dev].reshape(-1)
+    worst = results[tiles_dev : tiles_dev + 1, : pair_count // halves]
+    return peak, worst
 
 
 def solution(mesh):

time: 23.4 us -> 19.5 us (0.83)
  local copies, waits for them, and re-layouts: 6.29 us -> 2.45 us
    unnamed x22 -> x0, local copies, waits for them, and re-layouts: 6.29 us -> none
    reshape x0 -> x1, local copies, waits for them, and re-layouts: none -> 1.26 us  [body(): peak = results[:tiles_dev].reshape(-1)]
    slice x0 -> x1, local copies, waits for them, and re-layouts: none -> 1.2 us  [body(): worst = results[tiles_dev:tiles_dev + 1, :pair_count // halves]]
where the time goes in v2:
time: 19.5 us; the launch traced here: 19.3 us
  Pallas kernels  16.2 us (83%)
  local copies, waits for them, and re-layouts  2.45 us (13%)
  between operations  0.64 us (3%)
    pallas_call x1, Pallas kernels, body(): pl.pallas_call(functools.partial(kernel, blocks, halves), out_shape=jax.S...  16.2 us
    reshape x1, local copies, waits for them, and re-layouts, body(): peak = results[:tiles_dev].reshape(-1)  1.26 us
    slice x1, local copies, waits for them, and re-layouts, body(): worst = results[tiles_dev:tiles_dev + 1, :pair_count // halves]  1.2 us

profile of v2, /device:TPU:0, one launch (start us, length us, event | category | flops | bytes accessed | tf_op | source)
XLA Modules:
  0.0 19.3 jit_solution(14470737810431750508)
XLA Ops:
  0.6 16.2 %screen.1 = f32[8,128]{1,0:T(8,128)} custom-call(s32[2,128]{1,0:T(2,128)} %bitcast.15, bf16[128,128]{1,0:T(8,128)(2,1)} %bitcast.9, s32[1,128]{1,0:T(1,128)} %out_ids_hbm.1, f32[8,128]{1,0:T(8,128)} %bitcast.10, s32[4,128]{1,0:T(4,128)} %bitcast.14, f32[8,128]{1,0:T(8,128)} %bitcast.11, f32[8,128]{1,0:T(8,128)} %bitcast.12, f32[8,128]{1,0:T(8,128)} %bitcast.13, ...), custom_call_target="tpu_custom_call" | custom-call | tf_op jit(solution)/shard_map/screen/pallas_call | solution.py:336
  16.8 1.2 %slice.7 = f32[1,64]{1,0:T(1,128)} slice(f32[8,128]{1,0:T(8,128)} %screen.1), slice={[4:5], [0:64]} | slice | bytes 512 | tf_op jit(solution)/shard_map/slice | solution.py:367
  18.0 1.3 %slice_bitcast_fusion = f32[512]{0:T(512)} fusion(f32[8,128]{1,0:T(8,128)} %screen.1), kind=kLoop, calls=%fused_computation | loop fusion | bytes 4096 | tf_op jit(solution)/shard_map/reshape | solution.py:366

commit v3 on v2

--- a/solution.py
+++ b/solution.py
@@ -154,12 +154,12 @@
     pl.semaphore_wait(barrier, devices - 1)
 
     def pair_copy(i):
-        other, where_to = place(i)
+        _, where_to = place(i)
         return pltpu.make_async_remote_copy(
             src_ref=pair_out,
             dst_ref=pair_in.at[me],
-            send_sem=pair_send.at[other],
-            recv_sem=pair_recv.at[me],
+            send_sem=pair_send,
+            recv_sem=pair_recv,
             device_id=where_to,
             device_id_type=MESH,
         )
@@ -172,8 +172,8 @@
         device_id={"state": 1 - state},
         device_id_type=MESH,
     )
+    table_copy.start()
     each(devices - 1, lambda i: pair_copy(i).start(), unrolled)
-    table_copy.start()
     pair_in[me] = pair_out[...]
 
     react_own = lookup(react_ref[...], high, low, own_row)
@@ -207,18 +207,8 @@
         worst = jnp.maximum(worst, jnp.where(absent, base_peak, 0.0))
     loads[9].wait()
 
-    def pair_arrived(i):
-        other, where_to = place(i)
-        pltpu.make_async_remote_copy(
-            src_ref=pair_out,
-            dst_ref=pair_in.at[other],
-            send_sem=pair_send.at[other],
-            recv_sem=pair_recv.at[other],
-            device_id=where_to,
-            device_id_type=MESH,
-        ).wait_recv()
-
-    each(devices - 1, pair_arrived, unrolled)
+    peers = pl.ds(0, devices - 1)
+    pltpu.make_async_copy(pair_in.at[peers], pair_in.at[peers], pair_recv).wait()
     flow_first = pair_in[0:blocks, 0] + pair_in[blocks:, 0]
     flow_second = pair_in[0:blocks, 1] + pair_in[blocks:, 1]
     first_all = pair_in[0:blocks, 2].astype(jnp.int32)
@@ -260,12 +250,12 @@
     worst_out[:, 0] = worst
 
     def worst_copy(i):
-        other, where_to = place(i)
+        _, where_to = place(i)
         return pltpu.make_async_remote_copy(
             src_ref=worst_out.at[where_to["blk"]],
             dst_ref=worst_in.at[me],
-            send_sem=worst_send.at[other],
-            recv_sem=worst_recv.at[me],
+            send_sem=worst_send,
+            recv_sem=worst_recv,
             device_id=where_to,
             device_id_type=MESH,
         )
@@ -276,29 +266,13 @@
         most = jnp.max(squares[t].T, axis=0, keepdims=True)
         out_ref[t : t + 1] = jnp.sqrt((most + rows[8 + t : 9 + t]) * rows[16 + t : 17 + t])
 
-    def worst_arrived(i):
-        other, where_to = place(i)
-        pltpu.make_async_remote_copy(
-            src_ref=worst_out.at[blk],
-            dst_ref=worst_in.at[other],
-            send_sem=worst_send.at[other],
-            recv_sem=worst_recv.at[other],
-            device_id=where_to,
-            device_id_type=MESH,
-        ).wait_recv()
-
-    each(devices - 1, worst_arrived, unrolled)
+    table_copy.wait_send()
+    pltpu.make_async_copy(pair_in.at[peers], pair_in.at[peers], pair_send).wait()
+    pltpu.make_async_copy(worst_in.at[peers], worst_in.at[peers], worst_send).wait()
+    pltpu.make_async_copy(worst_in.at[peers], worst_in.at[peers], worst_recv).wait()
     total = jnp.sqrt(jnp.max(worst_in[...], axis=0))
     half = pair_count // halves
     out_ref[tiles_dev : tiles_dev + 1, :half] = jnp.where(is_first, total[:, :half], total[:, half:])
-
-    table_copy.wait_send()
-
-    def sent(i):
-        pair_copy(i).wait_send()
-        worst_copy(i).wait_send()
-
-    each(devices - 1, sent, unrolled)
 
 
 def body(
@@ -353,16 +327,16 @@
             pltpu.VMEM((devices, 1, pair_count), f32),
             pltpu.SemaphoreType.DMA((10,)),
             pltpu.SemaphoreType.DMA((2,)),
-            pltpu.SemaphoreType.DMA((devices,)),
-            pltpu.SemaphoreType.DMA((devices,)),
-            pltpu.SemaphoreType.DMA((devices,)),
-            pltpu.SemaphoreType.DMA((devices,)),
+            pltpu.SemaphoreType.DMA(()),
+            pltpu.SemaphoreType.DMA(()),
+            pltpu.SemaphoreType.DMA(()),
+            pltpu.SemaphoreType.DMA(()),
         ],
         compiler_params=pltpu.CompilerParams(
-            collective_id=0, has_side_effects=True, vmem_limit_bytes=64 * 1024 * 1024
+            collective_id=0, has_side_effects=True, vmem_limit_bytes=48 * 1024 * 1024
         ),
         name="screen",
-    )(*operands)
+    )(*[pltpu.with_memory_space_constraint(x, pltpu.HBM) for x in operands])
     peak = results[:tiles_dev].reshape(-1)
     worst = results[tiles_dev : tiles_dev + 1, : pair_count // halves]
     return peak, worst

time: 19.5 us -> 16.8 us (0.86)
  local copies, waits for them, and re-layouts: 2.45 us -> 1.09 us
  Pallas kernels: 16.2 us -> 15 us
    pallas_call x1, Pallas kernels: 16.2 us -> 15 us  [body(): pl.pallas_call(functools.partial(kernel, blocks, halves), out_shape=jax.S...]
    slice x1, local copies, waits for them, and re-layouts: 1.2 us -> 0.51 us  [body(): worst = results[tiles_dev:tiles_dev + 1, :pair_count // halves]]
    reshape x1, local copies, waits for them, and re-layouts: 1.26 us -> 0.58 us  [body(): peak = results[:tiles_dev].reshape(-1)]
where the time goes in v3:
time: 16.8 us; the launch traced here: 16.7 us
  Pallas kernels  15 us (89%)
  local copies, waits for them, and re-layouts  1.09 us (6%)
  between operations  0.64 us (4%)
    pallas_call x1, Pallas kernels, body(): pl.pallas_call(functools.partial(kernel, blocks, halves), out_shape=jax.S...  15 us
    reshape x1, local copies, waits for them, and re-layouts, body(): peak = results[:tiles_dev].reshape(-1)  0.58 us
    slice x1, local copies, waits for them, and re-layouts, body(): worst = results[tiles_dev:tiles_dev + 1, :pair_count // halves]  0.51 us

profile of v3, /device:TPU:0, one launch (start us, length us, event | category | flops | bytes accessed | tf_op | source)
XLA Modules:
  0.0 16.7 jit_solution(13994919060537966047)
XLA Ops:
  0.6 15.0 %screen.1 = f32[8,128]{1,0:T(8,128)S(1)} custom-call(s32[2,128]{1,0:T(2,128)} %bitcast.15, bf16[128,128]{1,0:T(8,128)(2,1)} %bitcast.9, s32[1,128]{1,0:T(1,128)} %out_ids_hbm.1, f32[8,128]{1,0:T(8,128)} %bitcast.10, s32[4,128]{1,0:T(4,128)} %bitcast.14, f32[8,128]{1,0:T(8,128)} %bitcast.11, f32[8,128]{1,0:T(8,128)} %bitcast.12, f32[8,128]{1,0:T(8,128)} %bitcast.13, ...), custom_call_target="tpu_custom_call" | custom-call | tf_op jit(solution)/shard_map/screen/pallas_call | solution.py:310
  15.6 0.5 %slice.7 = f32[1,64]{1,0:T(1,128)} slice(f32[8,128]{1,0:T(8,128)S(1)} %screen.1), slice={[4:5], [0:64]} | slice | bytes 512 | tf_op jit(solution)/shard_map/slice | solution.py:341
  16.1 0.6 %slice_bitcast_fusion = f32[512]{0:T(512)} fusion(f32[8,128]{1,0:T(8,128)S(1)} %screen.1), kind=kLoop, calls=%fused_computation | loop fusion | bytes 4096 | tf_op jit(solution)/shard_map/reshape | solution.py:340

commit v4 on v3

--- a/solution.py
+++ b/solution.py
@@ -21,19 +21,6 @@
     for r in range(table.shape[0]):
         found = jnp.where(high == first_row + r, take_lanes(table[r : r + 1], low), found)
     return found
-
-
-def each(count, step, unrolled):
-    if unrolled:
-        for i in range(count):
-            step(i)
-    else:
-
-        def one(i, carry):
-            step(i)
-            return carry
-
-        lax.fori_loop(0, count, one, 0)
 
 
 def kernel(
@@ -49,7 +36,8 @@
     rating_hbm,
     ids_hbm,
     tiles_hbm,
-    out_ref,
+    peak_ref,
+    worst_ref,
     pairs_ref,
     coup_ref,
     out_ids_ref,
@@ -68,7 +56,9 @@
     weights,
     columns,
     rows,
+    pair_rows,
     squares,
+    tops,
     worst_out,
     worst_in,
     load_sems,
@@ -81,14 +71,21 @@
     devices = blocks * halves
     tiles_dev, slots, tile_size, _ = tiles_hbm.shape
     table_rows = real_ref.shape[0]
-    unrolled = devices <= 16
     blk = lax.axis_index("blk")
     state = lax.axis_index("state")
     me = state * blocks + blk
 
-    def place(i):
-        other = lax.rem(me + i + 1, devices)
-        return other, {"blk": lax.rem(other, blocks), "state": other // blocks}
+    def each_peer(step):
+        step(blk, 1 - state)
+
+        def one_block(i, carry):
+            turned = blk + i
+            to = jnp.where(turned >= blocks, turned - blocks, turned)
+            step(to, state)
+            step(to, 1 - state)
+            return carry
+
+        lax.fori_loop(1, blocks, one_block, 0)
 
     loads = [
         pltpu.make_async_copy(source, target, load_sems.at[i])
@@ -111,11 +108,11 @@
         load.start()
     barrier = pltpu.get_barrier_semaphore()
 
-    def greet(i):
-        _, where_to = place(i)
-        pl.semaphore_signal(barrier, inc=1, device_id=where_to, device_id_type=MESH)
-
-    each(devices - 1, greet, unrolled)
+    def greet(to, half):
+        there = {"blk": to, "state": half}
+        pl.semaphore_signal(barrier, inc=1, device_id=there, device_id_type=MESH)
+
+    each_peer(greet)
     for load in loads[8:]:
         load.start()
     for load in loads[:8]:
@@ -153,16 +150,15 @@
 
     pl.semaphore_wait(barrier, devices - 1)
 
-    def pair_copy(i):
-        _, where_to = place(i)
-        return pltpu.make_async_remote_copy(
+    def send_pairs(to, half):
+        pltpu.make_async_remote_copy(
             src_ref=pair_out,
             dst_ref=pair_in.at[me],
             send_sem=pair_send,
             recv_sem=pair_recv,
-            device_id=where_to,
+            device_id={"blk": to, "state": half},
             device_id_type=MESH,
-        )
+        ).start()
 
     table_copy = pltpu.make_async_remote_copy(
         src_ref=table_out,
@@ -173,7 +169,7 @@
         device_id_type=MESH,
     )
     table_copy.start()
-    each(devices - 1, lambda i: pair_copy(i).start(), unrolled)
+    each_peer(send_pairs)
     pair_in[me] = pair_out[...]
 
     react_own = lookup(react_ref[...], high, low, own_row)
@@ -197,36 +193,44 @@
             columns[t, q] = jnp.broadcast_to(column, (tile_size, pair_count))
     loads[8].wait()
     block_of = lax.broadcasted_iota(jnp.int32, (blocks, pair_count), 0)
-    worst = jnp.zeros((blocks, pair_count), jnp.float32)
-    for t in range(tiles_dev):
+
+    def base_tile(t, worst):
         base = columns[t, 0]
         base_peak = jnp.max((base * base + columns[t, 1]) * columns[t, 2], axis=0, keepdims=True)
         absent = block_of >= 0
         for k in range(slots):
             absent = absent & (block_of != ids_ref[t, k])
-        worst = jnp.maximum(worst, jnp.where(absent, base_peak, 0.0))
+        return jnp.maximum(worst, jnp.where(absent, base_peak, 0.0))
+
+    worst = lax.fori_loop(0, tiles_dev, base_tile, jnp.zeros((blocks, pair_count), jnp.float32))
     loads[9].wait()
 
     peers = pl.ds(0, devices - 1)
     pltpu.make_async_copy(pair_in.at[peers], pair_in.at[peers], pair_recv).wait()
     flow_first = pair_in[0:blocks, 0] + pair_in[blocks:, 0]
     flow_second = pair_in[0:blocks, 1] + pair_in[blocks:, 1]
-    first_all = pair_in[0:blocks, 2].astype(jnp.int32)
-    second_all = pair_in[0:blocks, 3].astype(jnp.int32)
     s_fs, s_sf = pair_in[blocks:, 2], pair_in[blocks:, 3]
     determinant = 1.0 - s_fs * s_sf
     w_first = (flow_first + s_fs * flow_second) / determinant
     w_second = (flow_second + s_sf * flow_first) / determinant
-    for b in range(blocks):
-        one_row = slice(b, b + 1)
+    pair_rows[0] = pair_in[0:blocks, 2]
+    pair_rows[1] = pair_in[0:blocks, 3]
+    pair_rows[2] = w_first
+    pair_rows[3] = w_second
+    place = spot.astype(jnp.float32)
+
+    def build(b, carry):
+        one_row = pl.ds(b, 1)
         weights[b + 1] = jnp.where(
-            spot == first_all[one_row],
-            w_first[one_row],
-            jnp.where(spot == second_all[one_row], w_second[one_row], 0.0),
+            place == pair_rows[0, one_row],
+            pair_rows[2, one_row],
+            jnp.where(place == pair_rows[1, one_row], pair_rows[3, one_row], 0.0),
         ).astype(jnp.bfloat16)
-
-    for t in range(tiles_dev):
-
+        return carry
+
+    lax.fori_loop(0, blocks, build, 0)
+
+    def one_tile(t, worst):
         def one_slot(k, carried):
             most, worst = carried
             block = ids_ref[t, k]
@@ -245,34 +249,49 @@
                 carried = one_slot(k, carried)
         else:
             carried = lax.fori_loop(0, slots, one_slot, carried)
-        most, worst = carried
-        squares[t] = most
+        squares[t] = carried[0]
+        return carried[1]
+
+    worst = lax.fori_loop(0, tiles_dev, one_tile, worst)
     worst_out[:, 0] = worst
 
-    def worst_copy(i):
-        _, where_to = place(i)
-        return pltpu.make_async_remote_copy(
-            src_ref=worst_out.at[where_to["blk"]],
+    def send_worst(to, half):
+        pltpu.make_async_remote_copy(
+            src_ref=worst_out.at[to],
             dst_ref=worst_in.at[me],
             send_sem=worst_send,
             recv_sem=worst_recv,
-            device_id=where_to,
+            device_id={"blk": to, "state": half},
             device_id_type=MESH,
-        )
-
-    each(devices - 1, lambda i: worst_copy(i).start(), unrolled)
+        ).start()
+
+    each_peer(send_worst)
     worst_in[me] = worst_out[blk]
-    for t in range(tiles_dev):
-        most = jnp.max(squares[t].T, axis=0, keepdims=True)
-        out_ref[t : t + 1] = jnp.sqrt((most + rows[8 + t : 9 + t]) * rows[16 + t : 17 + t])
-
+
+    def tile_peak(t, carry):
+        tops[pl.ds(t, 1)] = jnp.max(squares[t].T, axis=0, keepdims=True)
+        return carry
+
+    lax.fori_loop(0, tiles_dev, tile_peak, 0)
+    peak_ref[...] = jnp.sqrt((tops[0:tiles_dev] + rows[8 : 8 + tiles_dev]) * rows[16 : 16 + tiles_dev])
     table_copy.wait_send()
     pltpu.make_async_copy(pair_in.at[peers], pair_in.at[peers], pair_send).wait()
     pltpu.make_async_copy(worst_in.at[peers], worst_in.at[peers], worst_send).wait()
     pltpu.make_async_copy(worst_in.at[peers], worst_in.at[peers], worst_recv).wait()
     total = jnp.sqrt(jnp.max(worst_in[...], axis=0))
     half = pair_count // halves
-    out_ref[tiles_dev : tiles_dev + 1, :half] = jnp.where(is_first, total[:, :half], total[:, half:])
+    worst_ref[...] = jnp.where(is_first, total[:, :half], total[:, half:])
+
+
+def write_out(peak_ref, worst_ref, peak_hbm, worst_hbm, sems):
+    copies = (
+        pltpu.make_async_copy(peak_ref, peak_hbm, sems.at[0]),
+        pltpu.make_async_copy(worst_ref, worst_hbm, sems.at[1]),
+    )
+    for copy in copies:
+        copy.start()
+    for copy in copies:
+        copy.wait()
 
 
 def body(
@@ -307,11 +326,16 @@
         tile_values,
     )
     spaces = [pltpu.VMEM] * 8 + [pltpu.SMEM, pltpu.VMEM]
+    shapes = (
+        jax.ShapeDtypeStruct((tiles_dev, tile_size), f32),
+        jax.ShapeDtypeStruct((1, pair_count // halves), f32),
+    )
+    vmem = pl.BlockSpec(memory_space=pltpu.VMEM)
     results = pl.pallas_call(
         functools.partial(kernel, blocks, halves),
-        out_shape=jax.ShapeDtypeStruct((8, LANES), f32),
+        out_shape=shapes,
         in_specs=[pl.BlockSpec(memory_space=pltpu.HBM)] * 10,
-        out_specs=pl.BlockSpec(memory_space=pltpu.VMEM),
+        out_specs=(vmem, vmem),
         scratch_shapes=[space(x.shape, x.dtype) for space, x in zip(spaces, operands)]
         + [
             pltpu.VMEM((8, LANES), jnp.int32),
@@ -322,7 +346,9 @@
             pltpu.VMEM((blocks + 1, tile_size, pair_count), jnp.bfloat16),
             pltpu.VMEM((tiles_dev, 3, tile_size, pair_count), f32),
             pltpu.VMEM((LANES, LANES), f32),
+            pltpu.VMEM((4, blocks, pair_count), f32),
             pltpu.VMEM((tiles_dev, tile_size, pair_count), f32),
+            pltpu.VMEM((8, tile_size), f32),
             pltpu.VMEM((blocks, 1, pair_count), f32),
             pltpu.VMEM((devices, 1, pair_count), f32),
             pltpu.SemaphoreType.DMA((10,)),
@@ -337,9 +363,16 @@
         ),
         name="screen",
     )(*[pltpu.with_memory_space_constraint(x, pltpu.HBM) for x in operands])
-    peak = results[:tiles_dev].reshape(-1)
-    worst = results[tiles_dev : tiles_dev + 1, : pair_count // halves]
-    return peak, worst
+    hbm = pl.BlockSpec(memory_space=pltpu.HBM)
+    peak, worst = pl.pallas_call(
+        write_out,
+        out_shape=shapes,
+        in_specs=[vmem, vmem],
+        out_specs=(hbm, hbm),
+        scratch_shapes=[pltpu.SemaphoreType.DMA((2,))],
+        name="write_out",
+    )(*results)
+    return peak.reshape(-1), worst
 
 
 def solution(mesh):

time: 16.8 us -> 18.4 us (1.095)
  Pallas kernels: 15 us -> 16.5 us
    pallas_call x1 -> x2, Pallas kernels: 15 us -> 16.5 us  [the longest x1 15.3 us: body(): pl.pallas_call(functools.partial(kernel, blocks, halves), out_shape=shape...]
    unnamed x0 -> x4, local copies, waits for them, and re-layouts: none -> 1.08 us
    reshape x1 -> x0, local copies, waits for them, and re-layouts: 0.58 us -> none  [body(): peak = results[:tiles_dev].reshape(-1)]
    slice x1 -> x0, local copies, waits for them, and re-layouts: 0.51 us -> none  [body(): worst = results[tiles_dev:tiles_dev + 1, :pair_count // halves]]
where the time goes in v4:
time: 18.4 us; the launch traced here: 18.3 us
  Pallas kernels  16.5 us (90%)
  local copies, waits for them, and re-layouts  1.08 us (6%)
  between operations  0.65 us (4%)
    pallas_call x1, Pallas kernels, body(): pl.pallas_call(functools.partial(kernel, blocks, halves), out_shape=shape...  15.3 us
    pallas_call x1, Pallas kernels, body(): pl.pallas_call(write_out, out_shape=shapes, in_specs=[vmem, vmem], out_sp...  1.25 us
    unnamed x4, local copies, waits for them, and re-layouts  1.08 us

profile of v4, /device:TPU:0, one launch (start us, length us, event | category | flops | bytes accessed | tf_op | source)
XLA Modules:
  0.0 18.3 jit_solution(8679577537168791890)
XLA Ops:
  0.6 15.3 %screen.1 = (f32[4,128]{1,0:T(4,128)S(1)}, f32[1,64]{1,0:T(1,128)S(1)}) custom-call(s32[2,128]{1,0:T(2,128)} %bitcast.14, bf16[128,128]{1,0:T(8,128)(2,1)} %bitcast.8, s32[1,128]{1,0:T(1,128)} %out_ids_hbm.1, f32[8,128]{1,0:T(8,128)} %bitcast.9, s32[4,128]{1,0:T(4,128)} %bitcast.13, f32[8,128]{1,0:T(8,128)} %bitcast.10, f32[8,128]{1,0:T(8,128)} %bitcast.11, ...), custom_call_target="tpu_custom_call" | custom-call | tf_op jit(solution)/shard_map/screen/pallas_call | solution.py:334
  15.9 0.0 copy-start
  15.9 0.6 %copy-done = f32[4,128]{1,0:T(4,128)} copy-done((f32[4,128]{1,0:T(4,128)}, f32[4,128]{1,0:T(4,128)S(1)}, u32[]{:S(2)}) %copy-start) | copy-done | bytes 2072
  16.5 0.0 copy-start.1
  16.5 0.5 %copy-done.1 = f32[1,64]{1,0:T(1,128)} copy-done((f32[1,64]{1,0:T(1,128)}, f32[1,64]{1,0:T(1,128)S(1)}, u32[]{:S(2)}) %copy-start.1) | copy-done | bytes 280
  17.0 1.3 %write_out.1 = (f32[4,128]{1,0:T(4,128)}, f32[1,64]{1,0:T(1,128)}) custom-call(f32[4,128]{1,0:T(4,128)} %copy-done, f32[1,64]{1,0:T(1,128)} %copy-done.1), custom_call_target="tpu_custom_call" | custom-call | tf_op jit(solution)/shard_map/write_out/pallas_call | solution.py:367
Async XLA Ops:
  15.9 0.6 %copy-start = (f32[4,128]{1,0:T(4,128)}, f32[4,128]{1,0:T(4,128)S(1)}, u32[]{:S(2)}) copy-start(f32[4,128]{1,0:T(4,128)S(1)} %get-tuple-element.6.peak_ref) | copy-start | bytes 6148
  16.5 0.5 %copy-start.1 = (f32[1,64]{1,0:T(1,128)}, f32[1,64]{1,0:T(1,128)S(1)}, u32[]{:S(2)}) copy-start(f32[1,64]{1,0:T(1,128)S(1)} %get-tuple-element.7.worst_ref) | copy-start | bytes 772

commit v5 on v4

--- a/solution.py
+++ b/solution.py
@@ -56,9 +56,7 @@
     weights,
     columns,
     rows,
-    pair_rows,
     squares,
-    tops,
     worst_out,
     worst_in,
     load_sems,
@@ -76,6 +74,14 @@
     me = state * blocks + blk
 
     def each_peer(step):
+        if devices <= 16 and blocks & (blocks - 1) == 0:
+            turns = [2**j * (1 - 2 * ((blk // 2**j) % 2)) for j in range(blocks.bit_length() - 1)]
+            for apart in reversed(range(blocks)):
+                to = blk + sum(turn for j, turn in enumerate(turns) if apart >> j & 1)
+                step(to, 1 - state)
+                if apart:
+                    step(to, state)
+            return
         step(blk, 1 - state)
 
         def one_block(i, carry):
@@ -104,7 +110,7 @@
             )
         )
     ]
-    for load in loads[:8]:
+    for load in loads[:5]:
         load.start()
     barrier = pltpu.get_barrier_semaphore()
 
@@ -113,7 +119,7 @@
         pl.semaphore_signal(barrier, inc=1, device_id=there, device_id_type=MESH)
 
     each_peer(greet)
-    for load in loads[8:]:
+    for load in loads[5:]:
         load.start()
     for load in loads[:8]:
         load.wait()
@@ -193,44 +199,36 @@
             columns[t, q] = jnp.broadcast_to(column, (tile_size, pair_count))
     loads[8].wait()
     block_of = lax.broadcasted_iota(jnp.int32, (blocks, pair_count), 0)
-
-    def base_tile(t, worst):
+    worst = jnp.zeros((blocks, pair_count), jnp.float32)
+    for t in range(tiles_dev):
         base = columns[t, 0]
         base_peak = jnp.max((base * base + columns[t, 1]) * columns[t, 2], axis=0, keepdims=True)
         absent = block_of >= 0
         for k in range(slots):
             absent = absent & (block_of != ids_ref[t, k])
-        return jnp.maximum(worst, jnp.where(absent, base_peak, 0.0))
-
-    worst = lax.fori_loop(0, tiles_dev, base_tile, jnp.zeros((blocks, pair_count), jnp.float32))
+        worst = jnp.maximum(worst, jnp.where(absent, base_peak, 0.0))
     loads[9].wait()
 
     peers = pl.ds(0, devices - 1)
     pltpu.make_async_copy(pair_in.at[peers], pair_in.at[peers], pair_recv).wait()
     flow_first = pair_in[0:blocks, 0] + pair_in[blocks:, 0]
     flow_second = pair_in[0:blocks, 1] + pair_in[blocks:, 1]
+    first_all = pair_in[0:blocks, 2].astype(jnp.int32)
+    second_all = pair_in[0:blocks, 3].astype(jnp.int32)
     s_fs, s_sf = pair_in[blocks:, 2], pair_in[blocks:, 3]
     determinant = 1.0 - s_fs * s_sf
     w_first = (flow_first + s_fs * flow_second) / determinant
     w_second = (flow_second + s_sf * flow_first) / determinant
-    pair_rows[0] = pair_in[0:blocks, 2]
-    pair_rows[1] = pair_in[0:blocks, 3]
-    pair_rows[2] = w_first
-    pair_rows[3] = w_second
-    place = spot.astype(jnp.float32)
-
-    def build(b, carry):
-        one_row = pl.ds(b, 1)
+    for b in range(blocks):
+        one_row = slice(b, b + 1)
         weights[b + 1] = jnp.where(
-            place == pair_rows[0, one_row],
-            pair_rows[2, one_row],
-            jnp.where(place == pair_rows[1, one_row], pair_rows[3, one_row], 0.0),
+            spot == first_all[one_row],
+            w_first[one_row],
+            jnp.where(spot == second_all[one_row], w_second[one_row], 0.0),
         ).astype(jnp.bfloat16)
-        return carry
-
-    lax.fori_loop(0, blocks, build, 0)
-
-    def one_tile(t, worst):
+
+    for t in range(tiles_dev):
+
         def one_slot(k, carried):
             most, worst = carried
             block = ids_ref[t, k]
@@ -249,10 +247,8 @@
                 carried = one_slot(k, carried)
         else:
             carried = lax.fori_loop(0, slots, one_slot, carried)
-        squares[t] = carried[0]
-        return carried[1]
-
-    worst = lax.fori_loop(0, tiles_dev, one_tile, worst)
+        most, worst = carried
+        squares[t] = most
     worst_out[:, 0] = worst
 
     def send_worst(to, half):
@@ -267,13 +263,10 @@
 
     each_peer(send_worst)
     worst_in[me] = worst_out[blk]
-
-    def tile_peak(t, carry):
-        tops[pl.ds(t, 1)] = jnp.max(squares[t].T, axis=0, keepdims=True)
-        return carry
-
-    lax.fori_loop(0, tiles_dev, tile_peak, 0)
-    peak_ref[...] = jnp.sqrt((tops[0:tiles_dev] + rows[8 : 8 + tiles_dev]) * rows[16 : 16 + tiles_dev])
+    for t in range(tiles_dev):
+        most = jnp.max(squares[t].T, axis=0, keepdims=True)
+        peak_ref[t : t + 1] = jnp.sqrt((most + rows[8 + t : 9 + t]) * rows[16 + t : 17 + t])
+
     table_copy.wait_send()
     pltpu.make_async_copy(pair_in.at[peers], pair_in.at[peers], pair_send).wait()
     pltpu.make_async_copy(worst_in.at[peers], worst_in.at[peers], worst_send).wait()
@@ -346,9 +339,7 @@
             pltpu.VMEM((blocks + 1, tile_size, pair_count), jnp.bfloat16),
             pltpu.VMEM((tiles_dev, 3, tile_size, pair_count), f32),
             pltpu.VMEM((LANES, LANES), f32),
-            pltpu.VMEM((4, blocks, pair_count), f32),
             pltpu.VMEM((tiles_dev, tile_size, pair_count), f32),
-            pltpu.VMEM((8, tile_size), f32),
             pltpu.VMEM((blocks, 1, pair_count), f32),
             pltpu.VMEM((devices, 1, pair_count), f32),
             pltpu.SemaphoreType.DMA((10,)),
@@ -370,6 +361,7 @@
         in_specs=[vmem, vmem],
         out_specs=(hbm, hbm),
         scratch_shapes=[pltpu.SemaphoreType.DMA((2,))],
+        compiler_params=pltpu.CompilerParams(vmem_limit_bytes=2 * 1024 * 1024),
         name="write_out",
     )(*results)
     return peak.reshape(-1), worst

time: 18.4 us -> 16.1 us (0.88)
  Pallas kernels: 16.5 us -> 15.3 us
  local copies, waits for them, and re-layouts: 1.08 us -> 0 us
    unnamed x4 -> x0, local copies, waits for them, and re-layouts: 1.08 us -> none
    pallas_call x1, Pallas kernels: 1.25 us -> 0.6 us  [body(): pl.pallas_call(write_out, out_shape=shapes, in_specs=[vmem, vmem], out_sp...]
    pallas_call x1, Pallas kernels: 15.3 us -> 14.7 us  [body(): pl.pallas_call(functools.partial(kernel, blocks, halves), out_shape=shape...]
where the time goes in v5:
time: 16.1 us; the launch traced here: 16 us
  Pallas kernels  15.3 us (95%)
  between operations  0.64 us (4%)
    pallas_call x1, Pallas kernels, body(): pl.pallas_call(functools.partial(kernel, blocks, halves), out_shape=shape...  14.7 us
    pallas_call x1, Pallas kernels, body(): pl.pallas_call(write_out, out_shape=shapes, in_specs=[vmem, vmem], out_sp...  0.6 us

profile of v5, /device:TPU:0, one launch (start us, length us, event | category | flops | bytes accessed | tf_op | source)
XLA Modules:
  0.0 16.0 jit_solution(16779808914636008448)
XLA Ops:
  0.6 14.7 %screen.1 = (f32[4,128]{1,0:T(4,128)S(1)}, f32[1,64]{1,0:T(1,128)S(1)}) custom-call(s32[2,128]{1,0:T(2,128)} %bitcast.14, bf16[128,128]{1,0:T(8,128)(2,1)} %bitcast.8, s32[1,128]{1,0:T(1,128)} %out_ids_hbm.1, f32[8,128]{1,0:T(8,128)} %bitcast.9, s32[4,128]{1,0:T(4,128)} %bitcast.13, f32[8,128]{1,0:T(8,128)} %bitcast.10, f32[8,128]{1,0:T(8,128)} %bitcast.11, ...), custom_call_target="tpu_custom_call" | custom-call | tf_op jit(solution)/shard_map/screen/pallas_call | solution.py:327
  15.4 0.6 %write_out.1 = (f32[4,128]{1,0:T(4,128)}, f32[1,64]{1,0:T(1,128)}) custom-call(f32[4,128]{1,0:T(4,128)S(1)} %get-tuple-element.6.peak_ref, f32[1,64]{1,0:T(1,128)S(1)} %get-tuple-element.7.worst_ref), custom_call_target="tpu_custom_call" | custom-call | tf_op jit(solution)/shard_map/write_out/pallas_call | solution.py:358

commit v6 on v5

--- a/solution.py
+++ b/solution.py
@@ -110,8 +110,6 @@
             )
         )
     ]
-    for load in loads[:5]:
-        load.start()
     barrier = pltpu.get_barrier_semaphore()
 
     def greet(to, half):
@@ -119,7 +117,7 @@
         pl.semaphore_signal(barrier, inc=1, device_id=there, device_id_type=MESH)
 
     each_peer(greet)
-    for load in loads[5:]:
+    for load in loads:
         load.start()
     for load in loads[:8]:
         load.wait()
@@ -213,19 +211,24 @@
     pltpu.make_async_copy(pair_in.at[peers], pair_in.at[peers], pair_recv).wait()
     flow_first = pair_in[0:blocks, 0] + pair_in[blocks:, 0]
     flow_second = pair_in[0:blocks, 1] + pair_in[blocks:, 1]
-    first_all = pair_in[0:blocks, 2].astype(jnp.int32)
-    second_all = pair_in[0:blocks, 3].astype(jnp.int32)
+    first_all, second_all = pair_in[0:blocks, 2], pair_in[0:blocks, 3]
+    places = spot.astype(jnp.float32).astype(jnp.bfloat16).reshape(tile_size // 16, 16, pair_count)
     s_fs, s_sf = pair_in[blocks:, 2], pair_in[blocks:, 3]
     determinant = 1.0 - s_fs * s_sf
     w_first = (flow_first + s_fs * flow_second) / determinant
     w_second = (flow_second + s_sf * flow_first) / determinant
+    packed = (16, pair_count)
+
+    def spread(rows_all, b):
+        return jnp.broadcast_to(rows_all[b : b + 1], packed).astype(jnp.bfloat16)[None]
+
+    none = jnp.zeros((1, *packed), jnp.bfloat16)
     for b in range(blocks):
-        one_row = slice(b, b + 1)
         weights[b + 1] = jnp.where(
-            spot == first_all[one_row],
-            w_first[one_row],
-            jnp.where(spot == second_all[one_row], w_second[one_row], 0.0),
-        ).astype(jnp.bfloat16)
+            places == spread(first_all, b),
+            spread(w_first, b),
+            jnp.where(places == spread(second_all, b), spread(w_second, b), none),
+        ).reshape(tile_size, pair_count)
 
     for t in range(tiles_dev):
 

time: 16.1 us -> 16 us (level)
  no operation moved by 1% of the time
where the time goes in v6:
time: 16 us; the launch traced here: 15.9 us
  Pallas kernels  15.2 us (95%)
  between operations  0.64 us (4%)
    pallas_call x1, Pallas kernels, body(): pl.pallas_call(functools.partial(kernel, blocks, halves), out_shape=shape...  14.6 us
    pallas_call x1, Pallas kernels, body(): pl.pallas_call(write_out, out_shape=shapes, in_specs=[vmem, vmem], out_sp...  0.6 us

profile of v6, /device:TPU:0, one launch (start us, length us, event | category | flops | bytes accessed | tf_op | source)
XLA Modules:
  0.0 15.9 jit_solution(16317884064679682544)
XLA Ops:
  0.6 14.6 %screen.1 = (f32[4,128]{1,0:T(4,128)S(1)}, f32[1,64]{1,0:T(1,128)S(1)}) custom-call(s32[2,128]{1,0:T(2,128)} %bitcast.14, bf16[128,128]{1,0:T(8,128)(2,1)} %bitcast.8, s32[1,128]{1,0:T(1,128)} %out_ids_hbm.1, f32[8,128]{1,0:T(8,128)} %bitcast.9, s32[4,128]{1,0:T(4,128)} %bitcast.13, f32[8,128]{1,0:T(8,128)} %bitcast.10, f32[8,128]{1,0:T(8,128)} %bitcast.11, ...), custom_call_target="tpu_custom_call" | custom-call | tf_op jit(solution)/shard_map/screen/pallas_call | solution.py:330
  15.3 0.6 %write_out.1 = (f32[4,128]{1,0:T(4,128)}, f32[1,64]{1,0:T(1,128)}) custom-call(f32[4,128]{1,0:T(4,128)S(1)} %get-tuple-element.6.peak_ref, f32[1,64]{1,0:T(1,128)S(1)} %get-tuple-element.7.worst_ref), custom_call_target="tpu_custom_call" | custom-call | tf_op jit(solution)/shard_map/write_out/pallas_call | solution.py:361

commit v7 on v6

--- a/solution.py
+++ b/solution.py
@@ -148,16 +148,17 @@
     real_own = lookup(real_ref[...], high, low, own_row)
     flows = real_own[tiles_dev : tiles_dev + 2].astype(jnp.bfloat16).astype(jnp.float32)
     is_first = state == 0
-    pair_out[0:2] = flows
-    pair_out[2:3] = jnp.where(is_first, first.astype(jnp.float32), s_first_second)
-    pair_out[3:4] = jnp.where(is_first, second.astype(jnp.float32), s_second_first)
+    pair_out[0] = flows[0:1]
+    pair_out[1] = flows[1:2]
+    pair_out[2] = jnp.where(is_first, first.astype(jnp.float32), s_first_second)
+    pair_out[3] = jnp.where(is_first, second.astype(jnp.float32), s_second_first)
 
     pl.semaphore_wait(barrier, devices - 1)
 
     def send_pairs(to, half):
         pltpu.make_async_remote_copy(
             src_ref=pair_out,
-            dst_ref=pair_in.at[me],
+            dst_ref=pair_in.at[:, pl.ds(me, 1)],
             send_sem=pair_send,
             recv_sem=pair_recv,
             device_id={"blk": to, "state": half},
@@ -174,7 +175,7 @@
     )
     table_copy.start()
     each_peer(send_pairs)
-    pair_in[me] = pair_out[...]
+    pair_in[:, pl.ds(me, 1)] = pair_out[...]
 
     react_own = lookup(react_ref[...], high, low, own_row)
     limit_mine = lookup(limit_own, high, low, own_row)
@@ -208,12 +209,12 @@
     loads[9].wait()
 
     peers = pl.ds(0, devices - 1)
-    pltpu.make_async_copy(pair_in.at[peers], pair_in.at[peers], pair_recv).wait()
-    flow_first = pair_in[0:blocks, 0] + pair_in[blocks:, 0]
-    flow_second = pair_in[0:blocks, 1] + pair_in[blocks:, 1]
-    first_all, second_all = pair_in[0:blocks, 2], pair_in[0:blocks, 3]
+    pltpu.make_async_copy(pair_in.at[:, peers], pair_in.at[:, peers], pair_recv).wait()
+    flow_first = pair_in[0, 0:blocks] + pair_in[0, blocks:]
+    flow_second = pair_in[1, 0:blocks] + pair_in[1, blocks:]
+    first_all, second_all = pair_in[2, 0:blocks], pair_in[3, 0:blocks]
     places = spot.astype(jnp.float32).astype(jnp.bfloat16).reshape(tile_size // 16, 16, pair_count)
-    s_fs, s_sf = pair_in[blocks:, 2], pair_in[blocks:, 3]
+    s_fs, s_sf = pair_in[2, blocks:], pair_in[3, blocks:]
     determinant = 1.0 - s_fs * s_sf
     w_first = (flow_first + s_fs * flow_second) / determinant
     w_second = (flow_second + s_sf * flow_first) / determinant
@@ -252,12 +253,12 @@
             carried = lax.fori_loop(0, slots, one_slot, carried)
         most, worst = carried
         squares[t] = most
-    worst_out[:, 0] = worst
+    worst_out[...] = worst
 
     def send_worst(to, half):
         pltpu.make_async_remote_copy(
-            src_ref=worst_out.at[to],
-            dst_ref=worst_in.at[me],
+            src_ref=worst_out.at[pl.ds(to, 1)],
+            dst_ref=worst_in.at[pl.ds(me, 1)],
             send_sem=worst_send,
             recv_sem=worst_recv,
             device_id={"blk": to, "state": half},
@@ -265,16 +266,16 @@
         ).start()
 
     each_peer(send_worst)
-    worst_in[me] = worst_out[blk]
+    worst_in[pl.ds(me, 1)] = worst_out[pl.ds(blk, 1)]
     for t in range(tiles_dev):
         most = jnp.max(squares[t].T, axis=0, keepdims=True)
         peak_ref[t : t + 1] = jnp.sqrt((most + rows[8 + t : 9 + t]) * rows[16 + t : 17 + t])
 
     table_copy.wait_send()
-    pltpu.make_async_copy(pair_in.at[peers], pair_in.at[peers], pair_send).wait()
+    pltpu.make_async_copy(pair_in.at[:, peers], pair_in.at[:, peers], pair_send).wait()
     pltpu.make_async_copy(worst_in.at[peers], worst_in.at[peers], worst_send).wait()
     pltpu.make_async_copy(worst_in.at[peers], worst_in.at[peers], worst_recv).wait()
-    total = jnp.sqrt(jnp.max(worst_in[...], axis=0))
+    total = jnp.sqrt(jnp.max(worst_in[...], axis=0, keepdims=True))
     half = pair_count // halves
     worst_ref[...] = jnp.where(is_first, total[:, :half], total[:, half:])
 
@@ -337,14 +338,14 @@
             pltpu.VMEM((8, LANES), jnp.int32),
             pltpu.VMEM((3, table_rows, LANES), f32),
             pltpu.VMEM((3, table_rows, LANES), f32),
-            pltpu.VMEM((4, pair_count), f32),
-            pltpu.VMEM((devices, 4, pair_count), f32),
+            pltpu.VMEM((4, 1, pair_count), f32),
+            pltpu.VMEM((4, devices, pair_count), f32),
             pltpu.VMEM((blocks + 1, tile_size, pair_count), jnp.bfloat16),
             pltpu.VMEM((tiles_dev, 3, tile_size, pair_count), f32),
             pltpu.VMEM((LANES, LANES), f32),
             pltpu.VMEM((tiles_dev, tile_size, pair_count), f32),
-            pltpu.VMEM((blocks, 1, pair_count), f32),
-            pltpu.VMEM((devices, 1, pair_count), f32),
+            pltpu.VMEM((blocks, pair_count), f32),
+            pltpu.VMEM((devices, pair_count), f32),
             pltpu.SemaphoreType.DMA((10,)),
             pltpu.SemaphoreType.DMA((2,)),
             pltpu.SemaphoreType.DMA(()),

time: 16 us -> 16 us (level)
  no operation moved by 1% of the time
where the time goes in v7:
time: 16 us; the launch traced here: 15.9 us
  Pallas kernels  15.2 us (95%)
  between operations  0.64 us (4%)
    pallas_call x1, Pallas kernels, body(): pl.pallas_call(functools.partial(kernel, blocks, halves), out_shape=shape...  14.6 us
    pallas_call x1, Pallas kernels, body(): pl.pallas_call(write_out, out_shape=shapes, in_specs=[vmem, vmem], out_sp...  0.6 us

profile of v7, /device:TPU:0, one launch (start us, length us, event | category | flops | bytes accessed | tf_op | source)
XLA Modules:
  0.0 15.9 jit_solution(12462524048060901580)
XLA Ops:
  0.6 14.6 %screen.1 = (f32[4,128]{1,0:T(4,128)S(1)}, f32[1,64]{1,0:T(1,128)S(1)}) custom-call(s32[2,128]{1,0:T(2,128)} %bitcast.14, bf16[128,128]{1,0:T(8,128)(2,1)} %bitcast.8, s32[1,128]{1,0:T(1,128)} %out_ids_hbm.1, f32[8,128]{1,0:T(8,128)} %bitcast.9, s32[4,128]{1,0:T(4,128)} %bitcast.13, f32[8,128]{1,0:T(8,128)} %bitcast.10, f32[8,128]{1,0:T(8,128)} %bitcast.11, ...), custom_call_target="tpu_custom_call" | custom-call | tf_op jit(solution)/shard_map/screen/pallas_call | solution.py:331
  15.3 0.6 %write_out.1 = (f32[4,128]{1,0:T(4,128)}, f32[1,64]{1,0:T(1,128)}) custom-call(f32[4,128]{1,0:T(4,128)S(1)} %get-tuple-element.6.peak_ref, f32[1,64]{1,0:T(1,128)S(1)} %get-tuple-element.7.worst_ref), custom_call_target="tpu_custom_call" | custom-call | tf_op jit(solution)/shard_map/write_out/pallas_call | solution.py:362

commit v8 on v7

--- a/solution.py
+++ b/solution.py
@@ -110,6 +110,8 @@
             )
         )
     ]
+    for load in loads[:5]:
+        load.start()
     barrier = pltpu.get_barrier_semaphore()
 
     def greet(to, half):
@@ -117,9 +119,9 @@
         pl.semaphore_signal(barrier, inc=1, device_id=there, device_id_type=MESH)
 
     each_peer(greet)
-    for load in loads:
+    for load in loads[5:]:
         load.start()
-    for load in loads[:8]:
+    for load in loads[:5]:
         load.wait()
 
     first, second = pairs_ref[0:1], pairs_ref[1:2]
@@ -140,10 +142,6 @@
     index[tiles_dev + 1 : tiles_dev + 2] = take_lanes(out_ids, jnp.broadcast_to(second, wide))[0:1]
     high, low = index[...] >> 7, index[...] & (LANES - 1)
 
-    limit_own = volt_ref[...] * rating_ref[...]
-    table_out[0] = real_ref[...]
-    table_out[1] = react_ref[...]
-    table_out[2] = limit_own
     own_row = state * table_rows
     real_own = lookup(real_ref[...], high, low, own_row)
     flows = real_own[tiles_dev : tiles_dev + 2].astype(jnp.bfloat16).astype(jnp.float32)
@@ -173,8 +171,14 @@
         device_id={"state": 1 - state},
         device_id_type=MESH,
     )
+    each_peer(send_pairs)
+    for load in loads[5:8]:
+        load.wait()
+    limit_own = volt_ref[...] * rating_ref[...]
+    table_out[0] = real_ref[...]
+    table_out[1] = react_ref[...]
+    table_out[2] = limit_own
     table_copy.start()
-    each_peer(send_pairs)
     pair_in[:, pl.ds(me, 1)] = pair_out[...]
 
     react_own = lookup(react_ref[...], high, low, own_row)
@@ -233,24 +237,44 @@
 
     for t in range(tiles_dev):
 
-        def one_slot(k, carried):
-            most, worst = carried
-            block = ids_ref[t, k]
-            delta = jnp.dot(tiles[t, k], weights[block + 1], preferred_element_type=jnp.float32)
+        def absorb(k, delta, most, worst):
             post = columns[t, 0] + delta
             square = post * post
             ratio = (square + columns[t, 1]) * columns[t, 2]
             top = jnp.max(ratio, axis=0, keepdims=True)
-            worst = jnp.where(block_of == block, jnp.maximum(worst, top), worst)
+            worst = jnp.where(block_of == ids_ref[t, k], jnp.maximum(worst, top), worst)
             return jnp.maximum(most, square), worst
+
+        def two_slots(i, carried):
+            k = 2 * i
+            first_w, second_w = weights[ids_ref[t, k] + 1], weights[ids_ref[t, k + 1] + 1]
+            blank = jnp.zeros_like(first_w)
+            both = jnp.concatenate(
+                [
+                    jnp.concatenate([first_w, blank], axis=1),
+                    jnp.concatenate([blank, second_w], axis=1),
+                ],
+                axis=0,
+            )
+            held = jnp.concatenate([tiles[t, k], tiles[t, k + 1]], axis=1)
+            delta = jnp.dot(held, both, preferred_element_type=jnp.float32)
+            carried = absorb(k, delta[:, :pair_count], *carried)
+            return absorb(k + 1, delta[:, pair_count:], *carried)
+
+        def one_slot(k, carried):
+            weight = weights[ids_ref[t, k] + 1]
+            delta = jnp.dot(tiles[t, k], weight, preferred_element_type=jnp.float32)
+            return absorb(k, delta, *carried)
 
         base = columns[t, 0]
         carried = (base * base, worst)
         if slots <= 4:
-            for k in range(slots):
-                carried = one_slot(k, carried)
+            for i in range(slots // 2):
+                carried = two_slots(i, carried)
         else:
-            carried = lax.fori_loop(0, slots, one_slot, carried)
+            carried = lax.fori_loop(0, slots // 2, two_slots, carried)
+        if slots % 2:
+            carried = one_slot(slots - 1, carried)
         most, worst = carried
         squares[t] = most
     worst_out[...] = worst

time: 16 us -> 16 us (level)
  no operation moved by 1% of the time
where the time goes in v8:
time: 16 us; the launch traced here: 15.8 us
  Pallas kernels  15.2 us (95%)
  between operations  0.64 us (4%)
    pallas_call x1, Pallas kernels, body(): pl.pallas_call(functools.partial(kernel, blocks, halves), out_shape=shape...  14.6 us
    pallas_call x1, Pallas kernels, body(): pl.pallas_call(write_out, out_shape=shapes, in_specs=[vmem, vmem], out_sp...  0.6 us

profile of v8, /device:TPU:0, one launch (start us, length us, event | category | flops | bytes accessed | tf_op | source)
XLA Modules:
  0.0 15.8 jit_solution(398722919865704975)
XLA Ops:
  0.6 14.6 %screen.1 = (f32[4,128]{1,0:T(4,128)S(1)}, f32[1,64]{1,0:T(1,128)S(1)}) custom-call(s32[2,128]{1,0:T(2,128)} %bitcast.14, bf16[128,128]{1,0:T(8,128)(2,1)} %bitcast.8, s32[1,128]{1,0:T(1,128)} %out_ids_hbm.1, f32[8,128]{1,0:T(8,128)} %bitcast.9, s32[4,128]{1,0:T(4,128)} %bitcast.13, f32[8,128]{1,0:T(8,128)} %bitcast.10, f32[8,128]{1,0:T(8,128)} %bitcast.11, ...), custom_call_target="tpu_custom_call" | custom-call | tf_op jit(solution)/shard_map/screen/pallas_call | solution.py:355
  15.2 0.6 %write_out.1 = (f32[4,128]{1,0:T(4,128)}, f32[1,64]{1,0:T(1,128)}) custom-call(f32[4,128]{1,0:T(4,128)S(1)} %get-tuple-element.6.peak_ref, f32[1,64]{1,0:T(1,128)S(1)} %get-tuple-element.7.worst_ref), custom_call_target="tpu_custom_call" | custom-call | tf_op jit(solution)/shard_map/write_out/pallas_call | solution.py:386

commit v9 on v8

--- a/solution.py
+++ b/solution.py
@@ -146,10 +146,10 @@
     real_own = lookup(real_ref[...], high, low, own_row)
     flows = real_own[tiles_dev : tiles_dev + 2].astype(jnp.bfloat16).astype(jnp.float32)
     is_first = state == 0
-    pair_out[0] = flows[0:1]
-    pair_out[1] = flows[1:2]
-    pair_out[2] = jnp.where(is_first, first.astype(jnp.float32), s_first_second)
-    pair_out[3] = jnp.where(is_first, second.astype(jnp.float32), s_second_first)
+    determinant = 1.0 - s_first_second * s_second_first
+    pair_out[0] = (flows[0:1] + s_first_second * flows[1:2]) / determinant
+    pair_out[1] = (flows[1:2] + s_second_first * flows[0:1]) / determinant
+    pair_out[2] = jnp.where(is_first, first, second).astype(jnp.float32)
 
     pl.semaphore_wait(barrier, devices - 1)
 
@@ -214,14 +214,11 @@
 
     peers = pl.ds(0, devices - 1)
     pltpu.make_async_copy(pair_in.at[:, peers], pair_in.at[:, peers], pair_recv).wait()
-    flow_first = pair_in[0, 0:blocks] + pair_in[0, blocks:]
-    flow_second = pair_in[1, 0:blocks] + pair_in[1, blocks:]
-    first_all, second_all = pair_in[2, 0:blocks], pair_in[3, 0:blocks]
+    w_first = pair_in[0, 0:blocks] + pair_in[0, blocks:]
+    w_second = pair_in[1, 0:blocks] + pair_in[1, blocks:]
+    first_all, second_all = pair_in[2, 0:blocks], pair_in[2, blocks:]
     places = spot.astype(jnp.float32).astype(jnp.bfloat16).reshape(tile_size // 16, 16, pair_count)
-    s_fs, s_sf = pair_in[2, blocks:], pair_in[3, blocks:]
-    determinant = 1.0 - s_fs * s_sf
-    w_first = (flow_first + s_fs * flow_second) / determinant
-    w_second = (flow_second + s_sf * flow_first) / determinant
+
     packed = (16, pair_count)
 
     def spread(rows_all, b):
@@ -362,8 +359,8 @@
             pltpu.VMEM((8, LANES), jnp.int32),
             pltpu.VMEM((3, table_rows, LANES), f32),
             pltpu.VMEM((3, table_rows, LANES), f32),
-            pltpu.VMEM((4, 1, pair_count), f32),
-            pltpu.VMEM((4, devices, pair_count), f32),
+            pltpu.VMEM((3, 1, pair_count), f32),
+            pltpu.VMEM((3, devices, pair_count), f32),
             pltpu.VMEM((blocks + 1, tile_size, pair_count), jnp.bfloat16),
             pltpu.VMEM((tiles_dev, 3, tile_size, pair_count), f32),
             pltpu.VMEM((LANES, LANES), f32),

time: 16 us -> 16 us (level)
  no operation moved by 1% of the time
where the time goes in v9:
time: 16 us; the launch traced here: 15.8 us
  Pallas kernels  15.2 us (95%)
  between operations  0.64 us (4%)
    pallas_call x1, Pallas kernels, body(): pl.pallas_call(functools.partial(kernel, blocks, halves), out_shape=shape...  14.6 us
    pallas_call x1, Pallas kernels, body(): pl.pallas_call(write_out, out_shape=shapes, in_specs=[vmem, vmem], out_sp...  0.6 us

profile of v9, /device:TPU:0, one launch (start us, length us, event | category | flops | bytes accessed | tf_op | source)
XLA Modules:
  0.0 15.8 jit_solution(1756912232878750537)
XLA Ops:
  0.6 14.6 %screen.1 = (f32[4,128]{1,0:T(4,128)S(1)}, f32[1,64]{1,0:T(1,128)S(1)}) custom-call(s32[2,128]{1,0:T(2,128)} %bitcast.14, bf16[128,128]{1,0:T(8,128)(2,1)} %bitcast.8, s32[1,128]{1,0:T(1,128)} %out_ids_hbm.1, f32[8,128]{1,0:T(8,128)} %bitcast.9, s32[4,128]{1,0:T(4,128)} %bitcast.13, f32[8,128]{1,0:T(8,128)} %bitcast.10, f32[8,128]{1,0:T(8,128)} %bitcast.11, ...), custom_call_target="tpu_custom_call" | custom-call | tf_op jit(solution)/shard_map/screen/pallas_call | solution.py:352
  15.2 0.6 %write_out.1 = (f32[4,128]{1,0:T(4,128)}, f32[1,64]{1,0:T(1,128)}) custom-call(f32[4,128]{1,0:T(4,128)S(1)} %get-tuple-element.6.peak_ref, f32[1,64]{1,0:T(1,128)S(1)} %get-tuple-element.7.worst_ref), custom_call_target="tpu_custom_call" | custom-call | tf_op jit(solution)/shard_map/write_out/pallas_call | solution.py:383
